TPU v7x, 1024 devices: a whole 8x8x8 slice. The times are simulated.
1024 devices in a mesh: gx: 16 (over z_hi, x), gy: 8 (over z_lo, core), gz: 8 (over y).
Axes of the slice: x: 8, y: 8, z: 8 (z_hi: 2, z_lo: 4; z = z_hi * 4 + z_lo), core: 2. Of those that a mesh axis runs over, the one named last changes fastest.
Arguments:
- populations: float32 [19, 96, 48, 1024], P(None, 'gx', 'gy', 'gz'), may hold values from 0.01 to 0.2
- fluid_mask: int32 [96, 48, 1024], P('gx', 'gy', 'gz'), may hold values 0 or 1
- stencil_base: int32 [16, 8, 8, 3, 642], P('gx', 'gy', 'gz'), may hold values from -4 to 128, as said below
- offsets: float32 [16, 8, 8, 3, 642], P('gx', 'gy', 'gz'), may hold values from 0 to 1
- occupied_cell_slots: int32 [16, 8, 8], P('gx', 'gy', 'gz'), may hold values from 0 to 1, as said below
- triangles: int32 [1280, 3], replicated, may hold values from 0 to 641, as said below
Outputs:
- next_populations: float32 [19, 96, 48, 1024], P(None, 'gx', 'gy', 'gz')
- interpolated_vertex_velocity: float32 [16, 8, 8, 3, 642], P('gx', 'gy', 'gz')
Inputs may be any that keep to these rules, and one draw needn't show every extreme that they name: `stencil_base`: along every dimension the four stencil nodes lie at most 4 nodes outside the owning block, so they lie in that block or in blocks beside it; the vertices of one slot lie within 3 nodes of a common centre inside the block. The first occupied_cell_slots slots of a block hold cells; the others are empty. `triangles`: each row names three different vertices of a cell; every vertex is named by some row.
All inputs are finite; a program needn't handle non-finite values. No bound on the sum of `fluid_mask` on one device may be relied on, other than what follows from the above.
Results may differ from a plain program's by a relative error of at most 0.0003.
Values sent between devices are 32-bit elements; how exact they have to be, the bound alone decides.
A program may use at most 64 MiB of HBM per device.

v0:
```python
import math

import jax
import jax.numpy as jnp
from jax import lax
from jax.sharding import PartitionSpec as P

NV = 642


LATTICE = (
    (0, 0, 0),
    (1, 0, 0),
    (-1, 0, 0),
    (0, 1, 0),
    (0, -1, 0),
    (0, 0, 1),
    (0, 0, -1),
    (1, 1, 0),
    (-1, -1, 0),
    (1, -1, 0),
    (-1, 1, 0),
    (1, 0, 1),
    (-1, 0, -1),
    (1, 0, -1),
    (-1, 0, 1),
    (0, 1, 1),
    (0, -1, -1),
    (0, 1, -1),
    (0, -1, 1),
)
RELAX_TIME = 0.8
STIFFNESS = 0.1
REST_LENGTH = 4.0


def extended_2(array, sides, width):
    for axis, dim in sides:
        size, length = (lax.axis_size(axis), array.shape[dim])
        up = [(i, (i + 1) % size) for i in range(size - 1)]
        down = [(j, i) for i, j in up]
        last = lax.slice_in_dim(array, length - width, length, axis=dim)
        initial = lax.slice_in_dim(array, 0, width, axis=dim)
        before = lax.ppermute(last, axis, up)
        after = lax.ppermute(initial, axis, down)
        array = jnp.concatenate([before, array, after], axis=dim)
    return array


def lattice_weight(direction):
    if direction == 0:
        return 1.0 / 3.0
    if direction <= 6:
        return 1.0 / 18.0
    return 1.0 / 36.0


def opposite(direction):
    if direction == 0:
        return 0
    if direction % 2 == 1:
        return direction + 1
    return direction - 1


def moments(populations):
    density = jnp.sum(populations, axis=0)
    momentum = []
    for axis in range(3):
        running = jnp.zeros_like(density)
        for direction, vector in enumerate(LATTICE):
            if vector[axis] != 0:
                running = running + float(vector[axis]) * populations[direction]
        momentum.append(running)
    return (density, jnp.stack(momentum))


def collide(populations, density, momentum, vertex_forces):
    velocity = [(momentum[axis] + 0.5 * vertex_forces[axis]) / density for axis in range(3)]
    speed_squared = (
        velocity[0] * velocity[0] + velocity[1] * velocity[1] + velocity[2] * velocity[2]
    )
    factor = 1.0 - 0.5 / RELAX_TIME
    result = []
    for direction, vector in enumerate(LATTICE):
        weight = lattice_weight(direction)
        projection = jnp.zeros_like(density)
        force_dot = jnp.zeros_like(density)
        shift_dot = jnp.zeros_like(density)
        for axis in range(3):
            step = float(vector[axis])
            projection = projection + step * velocity[axis]
            force_dot = force_dot + step * vertex_forces[axis]
            shift_dot = shift_dot + (step - velocity[axis]) * vertex_forces[axis]
        equilibrium = (
            weight
            * density
            * (1.0 + 3.0 * projection + 4.5 * projection * projection - 1.5 * speed_squared)
        )
        source_term = factor * weight * (3.0 * shift_dot + 9.0 * projection * force_dot)
        result.append(
            populations[direction]
            - (populations[direction] - equilibrium) / RELAX_TIME
            + source_term
        )
    return jnp.stack(result)


def stream(collided, extended, fluid_ext):
    size_x, size_y, size_z = collided.shape[1:]
    arrived = []
    for direction, vector in enumerate(LATTICE):
        low_x, low_y, low_z = (1 - vector[0], 1 - vector[1], 1 - vector[2])
        source = extended[
            direction, low_x : low_x + size_x, low_y : low_y + size_y, low_z : low_z + size_z
        ]
        open_flag = fluid_ext[
            low_x : low_x + size_x, low_y : low_y + size_y, low_z : low_z + size_z
        ]
        arrived.append(jnp.where(open_flag > 0.5, source, collided[opposite(direction)]))
    return jnp.stack(arrived)


def kernel_weights(coordinate, corner_row, fraction_row):
    offset = coordinate[:, None] - corner_row[None, :]
    distance = offset.astype(jnp.float32) - 1.0 - fraction_row[None, :]
    inside = (offset >= 0) & (offset <= 3)
    return jnp.where(inside, 0.25 * (1.0 + jnp.cos(0.5 * math.pi * distance)), 0.0)


def compute_membrane_force(stencil_corner, corner_fraction, slot_alive_flags, triangles):
    position = (stencil_corner.astype(jnp.float32) + 1.0 + corner_fraction).reshape(3, -1, NV)
    vertex_forces = jnp.zeros_like(position)
    for first_corner, second_corner in ((0, 1), (1, 2), (2, 0)):
        anchor_pos = position[:, :, triangles[:, first_corner]]
        target_pos = position[:, :, triangles[:, second_corner]]
        edge_vector = target_pos - anchor_pos
        stretch = jnp.sum(edge_vector * edge_vector, axis=0) / (REST_LENGTH * REST_LENGTH)
        tension = STIFFNESS * (stretch - 1.0)[None] * edge_vector
        vertex_forces = vertex_forces.at[:, :, triangles[:, first_corner]].add(tension)
        vertex_forces = vertex_forces.at[:, :, triangles[:, second_corner]].add(-tension)
    return vertex_forces.reshape(3, -1) * slot_alive_flags[None, :]


def spread_block(stencil_corner, corner_fraction, vertex_load, extents):
    weight_x = kernel_weights(
        jnp.arange(extents[0], dtype=jnp.int32), stencil_corner[0], corner_fraction[0]
    )
    weight_y = kernel_weights(
        jnp.arange(extents[1], dtype=jnp.int32), stencil_corner[1], corner_fraction[1]
    )
    weight_z = kernel_weights(
        jnp.arange(extents[2], dtype=jnp.int32), stencil_corner[2], corner_fraction[2]
    )
    weighted = (
        weight_x[None, :, None, :] * weight_y[None, None, :, :] * vertex_load[:, None, None, :]
    )
    weighted = weighted.reshape(3 * extents[0] * extents[1], -1)
    spread_grid = jnp.dot(
        weighted, weight_z.T, precision=lax.Precision.HIGHEST, preferred_element_type=jnp.float32
    )
    return spread_grid.reshape(3, extents[0], extents[1], extents[2])


def interpolate_velocity(field, stencil_corner, corner_fraction, lower):
    extent_x, extent_y, extent_z = field.shape[1:]
    weight_x = kernel_weights(
        jnp.arange(extent_x, dtype=jnp.int32) + lower, stencil_corner[0], corner_fraction[0]
    )
    weight_y = kernel_weights(
        jnp.arange(extent_y, dtype=jnp.int32) + lower, stencil_corner[1], corner_fraction[1]
    )
    weight_z = kernel_weights(
        jnp.arange(extent_z, dtype=jnp.int32) + lower, stencil_corner[2], corner_fraction[2]
    )
    projected = jnp.dot(
        field.reshape(-1, extent_z),
        weight_z,
        precision=lax.Precision.HIGHEST,
        preferred_element_type=jnp.float32,
    )
    projected = projected.reshape(3, extent_x, extent_y, -1)
    return jnp.einsum(
        "cxyv,xv,yv->cv", projected, weight_x, weight_y, precision=lax.Precision.HIGHEST
    )


def on_device(populations, fluid_mask, stencil_base, offsets, occupied_cell_slots, triangles):
    block_x, block_y, block_z = populations.shape[1:]
    vertex_count = stencil_base.shape[-1]
    stencil_corner = stencil_base.reshape(3, vertex_count)
    corner_fraction = offsets.reshape(3, vertex_count)
    cell_slot_index = jnp.arange(vertex_count, dtype=jnp.int32) // NV
    slot_alive_flags = (cell_slot_index < occupied_cell_slots.reshape(())).astype(jnp.float32)
    density, momentum = moments(populations)
    flow_velocity = momentum / density[None]
    velocity_with_halo = extended_2(flow_velocity, (("gx", 1), ("gy", 2), ("gz", 3)), 4)
    interpolated_vertex_velocity = (
        interpolate_velocity(velocity_with_halo, stencil_corner, corner_fraction, -4)
        * slot_alive_flags[None, :]
    )
    local_vertex_load = compute_membrane_force(
        stencil_corner, corner_fraction, slot_alive_flags, triangles
    )
    packed = jnp.concatenate(
        [stencil_corner.astype(jnp.float32), corner_fraction, local_vertex_load], axis=0
    )
    neighbours = extended_2(
        packed.reshape(1, 1, 1, 9, vertex_count), (("gx", 0), ("gy", 1), ("gz", 2)), 1
    )

    def unpack(cell_record):
        return (cell_record[0:3].astype(jnp.int32), cell_record[3:6], cell_record[6:9])

    records = neighbours.reshape(27, -1, vertex_count)
    block_sizes = jnp.array([block_x, block_y, block_z], jnp.int32)

    def add_neighbour(running, carried):
        number, cell_record = carried
        their_corner, their_fraction, their_load = unpack(cell_record)
        relative = jnp.stack([number // 9, number // 3 % 3, number % 3]) - 1
        shifted = their_corner + (relative * block_sizes)[:, None]
        spread_grid = spread_block(shifted, their_fraction, their_load, (block_x, block_y, block_z))
        return (running + spread_grid, None)

    vertex_forces, _ = lax.scan(
        add_neighbour,
        jnp.zeros((3, block_x, block_y, block_z), jnp.float32),
        (jnp.arange(27, dtype=jnp.int32), records),
    )
    collided = collide(populations, density, momentum, vertex_forces)
    flags = fluid_mask.astype(jnp.float32)
    stacked = jnp.concatenate([collided, flags[None]], axis=0)
    extended = extended_2(stacked, (("gx", 1), ("gy", 2), ("gz", 3)), 1)
    next_populations = stream(collided, extended[:19], extended[19])
    return (next_populations, interpolated_vertex_velocity.reshape(1, 1, 1, 3, vertex_count))


def solution(mesh):
    placed = (
        P(None, "gx", "gy", "gz"),
        P("gx", "gy", "gz"),
        P("gx", "gy", "gz", None, None),
        P("gx", "gy", "gz", None, None),
        P("gx", "gy", "gz"),
        P(),
    )
    return jax.shard_map(
        on_device,
        mesh=mesh,
        in_specs=placed,
        out_specs=(P(None, "gx", "gy", "gz"), P("gx", "gy", "gz", None, None)),
        check_vma=False,
    )
```

profile of v0, /device:TPU:206, one launch (start us, length us, event | category | flops | bytes accessed | tf_op | source)
XLA Modules:
  0.0 350.3 jit_solution(14538207923474253654)
XLA Ops:
  12.6 9.5 %scatter_custom_fusion = f32[3,642]{0,1:T(8,128)S(1)} fusion(s32[1280]{0:T(1024)S(1)} %get-tuple-element.174, f32[1280]{0:T(1024)S(1)} %add_multiply_fusion.4, f32[]{:T(128)} %constant.176.clone.1, f32[1280,3]{1,0:T(8,128)S(1)} %gather_fusion, f32[1280,3]{1,0:T(8,128)S(1)} %gather_fusion.1), kind=kCustom, calls=%fused_computation.100 | custom fusion | flops 11520 | bytes 1326620 | tf_op jit(solution)/shard_map/scatter-add | solution.py:140
  22.2 9.6 %scatter_custom_fusion.1 = f32[3,642]{0,1:T(8,128)S(1)} fusion(f32[3,642]{0,1:T(8,128)S(1)} %scatter_custom_fusion, s32[1280]{0:T(1024)S(1)} %get-tuple-element.175, f32[1280]{0:T(1024)S(1)} %add_multiply_fusion.4, f32[1280,3]{1,0:T(8,128)S(1)} %gather_fusion, f32[1280,3]{1,0:T(8,128)S(1)} %gather_fusion.1), kind=kCustom, calls=%fused_computation.98 | custom fusion | flops 15360 | bytes 1326616 | tf_op jit(solution)/shard_map/scatter-add | solution.py:141
  31.8 9.6 %scatter_custom_fusion.2 = f32[3,642]{0,1:T(8,128)S(1)} fusion(f32[3,642]{0,1:T(8,128)S(1)} %scatter_custom_fusion.1, s32[1280]{0:T(1024)S(1)} %get-tuple-element.175, f32[1280]{0:T(1024)S(1)} %add_multiply_fusion.3, f32[1280,3]{1,0:T(8,128)S(1)} %gather_fusion.2, f32[1280,3]{1,0:T(8,128)S(1)} %gather_fusion), kind=kCustom, calls=%fused_computation.93 | custom fusion | flops 11520 | bytes 1326616 | tf_op jit(solution)/shard_map/scatter-add | solution.py:140
  41.4 9.8 %scatter_custom_fusion.3 = f32[3,642]{0,1:T(8,128)S(1)} fusion(f32[3,642]{0,1:T(8,128)S(1)} %scatter_custom_fusion.2, s32[1280]{0:T(1024)S(1)} %get-tuple-element.173, f32[1280]{0:T(1024)S(1)} %add_multiply_fusion.3, f32[1280,3]{1,0:T(8,128)S(1)} %gather_fusion.2, f32[1280,3]{1,0:T(8,128)S(1)} %gather_fusion), kind=kCustom, calls=%fused_computation.91 | custom fusion | flops 15360 | bytes 1326616 | tf_op jit(solution)/shard_map/scatter-add | solution.py:141
  51.1 9.6 %scatter_custom_fusion.4 = f32[3,642]{0,1:T(8,128)S(1)} fusion(f32[3,642]{0,1:T(8,128)S(1)} %scatter_custom_fusion.3, s32[1280]{0:T(1024)S(1)} %get-tuple-element.173, f32[1280]{0:T(1024)S(1)} %add_multiply_fusion.2, f32[1280,3]{1,0:T(8,128)S(1)} %gather_fusion.1, f32[1280,3]{1,0:T(8,128)S(1)} %gather_fusion.2), kind=kCustom, calls=%fused_computation.86 | custom fusion | flops 11520 | bytes 1326616 | tf_op jit(solution)/shard_map/scatter-add | solution.py:140
  60.8 9.6 %scatter_custom_fusion.5 = f32[3,642]{0,1:T(8,128)S(1)} fusion(f32[3,642]{0,1:T(8,128)S(1)} %scatter_custom_fusion.4, s32[1280]{0:T(1024)S(1)} %get-tuple-element.174, f32[1280]{0:T(1024)S(1)} %add_multiply_fusion.2, f32[1280,3]{1,0:T(8,128)S(1)} %gather_fusion.1, f32[1280,3]{1,0:T(8,128)S(1)} %gather_fusion.2), kind=kCustom, calls=%fused_computation.84 | custom fusion | flops 15360 | bytes 1326616 | tf_op jit(solution)/shard_map/scatter-add | solution.py:141
  70.6 3.3 collective-permute-start.1
  73.9 12.0 %collective-permute-start = (f32[1,1,1,9,642]{4,3,2,1,0:T(8,128)S(1)}, f32[1,1,1,9,642]{4,3,2,1,0:T(8,128)S(1)}, u32[]{:S(2)}, u32[]{:S(2)}) collective-permute-start(f32[1,1,1,9,642]{4,3,2,1,0:T(8,128)S(1)} %maximum_bitcast_fusion), channel_id=1, source_target_pairs={{0,64},{64,128},{128,192},{192,256},{256,320},{320,384},{384,448},... | collective-permute-start | bytes 69344 | tf_op jit(solution)/shard_map/ppermute | solution.py:44
  89.7 2.4 collective-permute-start.2
  92.2 3.3 collective-permute-done.2
  98.0 3.8 %collective-permute-start.4 = (f32[3,3,1,9,642]{4,2,3,1,0:T(1,128)S(1)}, f32[3,3,1,9,642]{4,2,3,1,0:T(1,128)S(1)}, u32[]{:S(2)}, u32[]{:S(2)}) collective-permute-start(f32[3,3,1,9,642]{4,2,3,1,0:T(1,128)S(1)} %pad_maximum_fusion.3), channel_id=1, source_target_pairs={{0,1},{1,2},{2,3},{3,4},{4,5},{5,6},{6,7},{8,9},{9,10},{10,11},{11... | collective-permute-start | bytes 624032 | tf_op jit(solution)/shard_map/ppermute | solution.py:44
  102.2 3.4 collective-permute-done.5
  105.7 3.2 collective-permute-done.4
  110.2 168.4 %while.15 = (s32[]{:T(128)}, f32[3,6,6,128]{3,2,1,0:T(8,128)S(1)}, f32[27,9,642]{2,1,0:T(8,128)S(1)}, s32[27]{0:T(128)S(1)}, s32[]{:T(128)}, /*index=5*/s32[]{:T...) while((s32[]{:T(128)}, f32[3,6,6,128]{3,2,1,0:T(8,128)S(1)}, ...), condition=%wide.region_11.12_spmd.clone.clone, body=%wide.region_10.11_spmd.sunk.clone.clone.sunk | while | flops 107612768 | bytes 442409 | solution.py:226
  279.6 10.3 %collective-permute-start.12 = (f32[3,4,6,128]{3,2,1,0:T(8,128)S(1)}, f32[3,4,6,128]{3,2,1,0:T(8,128)S(1)}, u32[]{:S(2)}, u32[]{:S(2)}) collective-permute-start(f32[3,4,6,128]{3,2,1,0:T(8,128)S(1)} %get-tuple-element.235), channel_id=1, source_target_pairs={{0,64},{64,128},{128,192},{192,256},{256,320},{320,384},{384,448},... | collective-permute-start | bytes 110600 | tf_op jit(solution)/shard_map/ppermute | solution.py:44
  291.8 10.0 %collective-permute-done.13 = f32[3,4,6,128]{3,2,1,0:T(8,128)S(1)} collective-permute-done((f32[3,4,6,128]{3,2,1,0:T(8,128)S(1)}, f32[3,4,6,128]{3,2,1,0:T(8,128)S(1)}, u32[]{:S(2)}, u32[]{:S(2)}) %collective-permute-start.13) | collective-permute-done | bytes 36896 | tf_op jit(solution)/shard_map/ppermute | solution.py:45
  303.9 3.6 %collective-permute-start.15 = (f32[3,14,4,128]{3,2,1,0:T(4,128)S(1)}, f32[3,14,4,128]{3,2,1,0:T(4,128)S(1)}, u32[]{:S(2)}, u32[]{:S(2)}) collective-permute-start(f32[3,14,4,128]{3,2,1,0:T(4,128)S(1)} %get-tuple-element.234), channel_id=1, source_target_pairs={{8,0},{16,8},{24,16},{32,24},{40,32},{48,40},{56,48},{9,1},{17,9},... | collective-permute-start | bytes 258056 | tf_op jit(solution)/shard_map/ppermute | solution.py:45
  309.5 3.9 %collective-permute-start.7 = (f32[20,1,6,128]{3,2,1,0:T(8,128)S(1)}, f32[20,1,6,128]{3,2,1,0:T(8,128)S(1)}, u32[]{:S(2)}, u32[]{:S(2)}) collective-permute-start(f32[20,1,6,128]{3,2,1,0:T(8,128)S(1)} %get-tuple-element.211), channel_id=1, source_target_pairs={{64,0},{128,64},{192,128},{256,192},{320,256},{384,320},{448,384},... | collective-permute-start | bytes 184328 | tf_op jit(solution)/shard_map/ppermute | solution.py:45
  316.1 4.7 %collective-permute-start.17 = (f32[3,14,14,4]{3,2,1,0:T(8,128)S(1)}, f32[3,14,14,4]{3,2,1,0:T(8,128)S(1)}, u32[]{:S(2)}, u32[]{:S(2)}) collective-permute-start(f32[3,14,14,4]{3,2,1,0:T(8,128)S(1)} %get-tuple-element.232), channel_id=1, source_target_pairs={{1,0},{2,1},{3,2},{4,3},{5,4},{6,5},{7,6},{9,8},{10,9},{11,10},{12... | collective-permute-start | bytes 28232 | tf_op jit(solution)/shard_map/ppermute | solution.py:45
  320.8 2.6 collective-permute-done.7
  325.4 3.6 %collective-permute-start.9 = (f32[20,8,1,128]{3,2,1,0:T(1,128)S(1)}, f32[20,8,1,128]{3,2,1,0:T(1,128)S(1)}, u32[]{:S(2)}, u32[]{:S(2)}) collective-permute-start(f32[20,8,1,128]{3,2,1,0:T(1,128)S(1)} %get-tuple-element.209), channel_id=1, source_target_pairs={{8,0},{16,8},{24,16},{32,24},{40,32},{48,40},{56,48},{9,1},{17,9},... | collective-permute-start | bytes 245768 | tf_op jit(solution)/shard_map/ppermute | solution.py:45
  329.1 3.7 %multiply_reduce_fusion = f32[642,3,14]{0,2,1:T(8,128)S(1)} fusion(f32[642,14]{0,1:T(8,128)S(1)} %get-tuple-element.238, f32[3,14,14,4]{3,2,1,0:T(8,128)S(1)} %collective-permute-done.17, f32[3,14,4,128]{3,2,1,0:T(4,128)S(1)} %collective-permute-done.15, f32[3,4,6,128]{3,2,1,0:T(8,128)S(1)} %collective-permute-done.13, ...), kind=kOutput, calls=%fused_computation.65 | convolution fusion | flops 618241728 | bytes 469360 | tf_op jit(solution)/shard_map/dot_general | solution.py:176
  334.4 4.6 %collective-permute-start.11 = (f32[20,8,8,1]{0,2,3,1:T(8,128)S(1)}, f32[20,8,8,1]{0,2,3,1:T(8,128)S(1)}, u32[]{:S(2)}, u32[]{:S(2)}) collective-permute-start(f32[20,8,8,1]{0,2,3,1:T(8,128)S(1)} %copy.206), channel_id=1, source_target_pairs={{1,0},{2,1},{3,2},{4,3},{5,4},{6,5},{7,6},{9,8},{10,9},{11,10},{12... | collective-permute-start | bytes 15368 | tf_op jit(solution)/shard_map/ppermute | solution.py:45
  341.8 4.2 %collective-permute-done.10 = f32[20,8,8,1]{0,2,3,1:T(8,128)S(1)} collective-permute-done((f32[20,8,8,1]{0,2,3,1:T(8,128)S(1)}, f32[20,8,8,1]{0,2,3,1:T(8,128)S(1)}, u32[]{:S(2)}, u32[]{:S(2)}) %collective-permute-start.10) | collective-permute-done | bytes 5152 | tf_op jit(solution)/shard_map/ppermute | solution.py:44
  (366 shorter events, 117.5 us)
Async XLA Ops:
  60.7 25.2 %copy-start.2 = (s32[1,1,1,3,642]{4,2,3,1,0:T(1,128)S(1)}, s32[1,1,1,3,642]{4,2,3,1,0:T(1,128)}, u32[]{:S(2)}) copy-start(s32[1,1,1,3,642]{4,2,3,1,0:T(1,128)} %param.11) | copy-start | bytes 23116
  60.7 25.3 %copy-start.1 = (f32[1,1,1,3,642]{4,2,3,1,0:T(1,128)S(1)}, f32[1,1,1,3,642]{4,2,3,1,0:T(1,128)}, u32[]{:S(2)}) copy-start(f32[1,1,1,3,642]{4,2,3,1,0:T(1,128)} %param.12) | copy-start | bytes 23116
  60.7 25.3 %copy-start = (f32[19,6,6,128]{3,0,2,1:T(8,128)S(1)}, f32[19,6,6,128]{3,0,2,1:T(8,128)}, u32[]{:S(2)}) copy-start(f32[19,6,6,128]{3,0,2,1:T(8,128)} %param.9) | copy-start | bytes 1050628
  70.6 17.2 %collective-permute-start.1 = (f32[1,1,1,9,642]{4,3,2,1,0:T(8,128)S(1)}, f32[1,1,1,9,642]{4,3,2,1,0:T(8,128)S(1)}, u32[]{:S(2)}, u32[]{:S(2)}) collective-permute-start(f32[1,1,1,9,642]{4,3,2,1,0:T(8,128)S(1)} %maximum_bitcast_fusion), channel_id=1, source_target_pairs={{64,0},{128,64},{192,128},{256,192},{320,256},{384,320},{448,384},... | collective-permute-start | bytes 69344 | tf_op jit(solution)/shard_map/ppermute | solution.py:45
  73.9 13.8 %collective-permute-start = (f32[1,1,1,9,642]{4,3,2,1,0:T(8,128)S(1)}, f32[1,1,1,9,642]{4,3,2,1,0:T(8,128)S(1)}, u32[]{:S(2)}, u32[]{:S(2)}) collective-permute-start(f32[1,1,1,9,642]{4,3,2,1,0:T(8,128)S(1)} %maximum_bitcast_fusion), channel_id=1, source_target_pairs={{0,64},{64,128},{128,192},{192,256},{256,320},{320,384},{384,448},... | collective-permute-start | bytes 69344 | tf_op jit(solution)/shard_map/ppermute | solution.py:44
  87.8 4.4 %collective-permute-start.3 = (f32[3,1,1,9,642]{4,2,3,1,0:T(1,128)S(1)}, f32[3,1,1,9,642]{4,2,3,1,0:T(1,128)S(1)}, u32[]{:S(2)}, u32[]{:S(2)}) collective-permute-start(f32[3,1,1,9,642]{4,2,3,1,0:T(1,128)S(1)} %constant_dynamic-update-slice_fusion), channel_id=1, source_target_pairs={{8,0},{16,8},{24,16},{32,24},{40,32},{48,40},{56,48},{9,1},{17,9},... | collective-permute-start | bytes 208016 | tf_op jit(solution)/shard_map/ppermute | solution.py:45
  89.7 5.8 %collective-permute-start.2 = (f32[3,1,1,9,642]{4,2,3,1,0:T(1,128)S(1)}, f32[3,1,1,9,642]{4,2,3,1,0:T(1,128)S(1)}, u32[]{:S(2)}, u32[]{:S(2)}) collective-permute-start(f32[3,1,1,9,642]{4,2,3,1,0:T(1,128)S(1)} %constant_dynamic-update-slice_fusion), channel_id=1, source_target_pairs={{0,8},{8,16},{16,24},{24,32},{32,40},{40,48},{48,56},{1,9},{9,17},... | collective-permute-start | bytes 208016 | tf_op jit(solution)/shard_map/ppermute | solution.py:44
  95.7 9.9 %collective-permute-start.5 = (f32[3,3,1,9,642]{4,2,3,1,0:T(1,128)S(1)}, f32[3,3,1,9,642]{4,2,3,1,0:T(1,128)S(1)}, u32[]{:S(2)}, u32[]{:S(2)}) collective-permute-start(f32[3,3,1,9,642]{4,2,3,1,0:T(1,128)S(1)} %pad_maximum_fusion.3), channel_id=1, source_target_pairs={{1,0},{2,1},{3,2},{4,3},{5,4},{6,5},{7,6},{9,8},{10,9},{11,10},{12... | collective-permute-start | bytes 624032 | tf_op jit(solution)/shard_map/ppermute | solution.py:45
  98.0 10.9 %collective-permute-start.4 = (f32[3,3,1,9,642]{4,2,3,1,0:T(1,128)S(1)}, f32[3,3,1,9,642]{4,2,3,1,0:T(1,128)S(1)}, u32[]{:S(2)}, u32[]{:S(2)}) collective-permute-start(f32[3,3,1,9,642]{4,2,3,1,0:T(1,128)S(1)} %pad_maximum_fusion.3), channel_id=1, source_target_pairs={{0,1},{1,2},{2,3},{3,4},{4,5},{5,6},{6,7},{8,9},{9,10},{10,11},{11... | collective-permute-start | bytes 624032 | tf_op jit(solution)/shard_map/ppermute | solution.py:44
  109.6 0.7 copy-start.4
  279.2 12.6 %copy-start.3 = (s32[6,6,128]{2,1,0:T(8,128)S(1)}, s32[6,6,128]{2,1,0:T(8,128)}, u32[]{:S(2)}) copy-start(s32[6,6,128]{2,1,0:T(8,128)} %param.10) | copy-start | bytes 55300
  279.6 12.2 %collective-permute-start.12 = (f32[3,4,6,128]{3,2,1,0:T(8,128)S(1)}, f32[3,4,6,128]{3,2,1,0:T(8,128)S(1)}, u32[]{:S(2)}, u32[]{:S(2)}) collective-permute-start(f32[3,4,6,128]{3,2,1,0:T(8,128)S(1)} %get-tuple-element.235), channel_id=1, source_target_pairs={{0,64},{64,128},{128,192},{192,256},{256,320},{320,384},{384,448},... | collective-permute-start | bytes 110600 | tf_op jit(solution)/shard_map/ppermute | solution.py:44
  289.9 12.0 %collective-permute-start.13 = (f32[3,4,6,128]{3,2,1,0:T(8,128)S(1)}, f32[3,4,6,128]{3,2,1,0:T(8,128)S(1)}, u32[]{:S(2)}, u32[]{:S(2)}) collective-permute-start(f32[3,4,6,128]{3,2,1,0:T(8,128)S(1)} %get-tuple-element.236), channel_id=1, source_target_pairs={{64,0},{128,64},{192,128},{256,192},{320,256},{384,320},{448,384},... | collective-permute-start | bytes 110600 | tf_op jit(solution)/shard_map/ppermute | solution.py:45
  301.9 11.5 %collective-permute-start.14 = (f32[3,14,4,128]{3,2,1,0:T(4,128)S(1)}, f32[3,14,4,128]{3,2,1,0:T(4,128)S(1)}, u32[]{:S(2)}, u32[]{:S(2)}) collective-permute-start(f32[3,14,4,128]{3,2,1,0:T(4,128)S(1)} %get-tuple-element.233), channel_id=1, source_target_pairs={{0,8},{8,16},{16,24},{24,32},{32,40},{40,48},{48,56},{1,9},{9,17},... | collective-permute-start | bytes 258056 | tf_op jit(solution)/shard_map/ppermute | solution.py:44
  303.9 9.5 %collective-permute-start.15 = (f32[3,14,4,128]{3,2,1,0:T(4,128)S(1)}, f32[3,14,4,128]{3,2,1,0:T(4,128)S(1)}, u32[]{:S(2)}, u32[]{:S(2)}) collective-permute-start(f32[3,14,4,128]{3,2,1,0:T(4,128)S(1)} %get-tuple-element.234), channel_id=1, source_target_pairs={{8,0},{16,8},{24,16},{32,24},{40,32},{48,40},{56,48},{9,1},{17,9},... | collective-permute-start | bytes 258056 | tf_op jit(solution)/shard_map/ppermute | solution.py:45
  307.5 13.2 %collective-permute-start.6 = (f32[20,1,6,128]{3,2,1,0:T(8,128)S(1)}, f32[20,1,6,128]{3,2,1,0:T(8,128)S(1)}, u32[]{:S(2)}, u32[]{:S(2)}) collective-permute-start(f32[20,1,6,128]{3,2,1,0:T(8,128)S(1)} %get-tuple-element.210), channel_id=1, source_target_pairs={{0,64},{64,128},{128,192},{192,256},{256,320},{320,384},{384,448},... | collective-permute-start | bytes 184328 | tf_op jit(solution)/shard_map/ppermute | solution.py:44
  309.5 13.9 %collective-permute-start.7 = (f32[20,1,6,128]{3,2,1,0:T(8,128)S(1)}, f32[20,1,6,128]{3,2,1,0:T(8,128)S(1)}, u32[]{:S(2)}, u32[]{:S(2)}) collective-permute-start(f32[20,1,6,128]{3,2,1,0:T(8,128)S(1)} %get-tuple-element.211), channel_id=1, source_target_pairs={{64,0},{128,64},{192,128},{256,192},{320,256},{384,320},{448,384},... | collective-permute-start | bytes 184328 | tf_op jit(solution)/shard_map/ppermute | solution.py:45
  313.7 15.4 %collective-permute-start.16 = (f32[3,14,14,4]{3,2,1,0:T(8,128)S(1)}, f32[3,14,14,4]{3,2,1,0:T(8,128)S(1)}, u32[]{:S(2)}, u32[]{:S(2)}) collective-permute-start(f32[3,14,14,4]{3,2,1,0:T(8,128)S(1)} %get-tuple-element.231), channel_id=1, source_target_pairs={{0,1},{1,2},{2,3},{3,4},{4,5},{5,6},{6,7},{8,9},{9,10},{10,11},{11... | collective-permute-start | bytes 28232 | tf_op jit(solution)/shard_map/ppermute | solution.py:44
  316.1 13.0 %collective-permute-start.17 = (f32[3,14,14,4]{3,2,1,0:T(8,128)S(1)}, f32[3,14,14,4]{3,2,1,0:T(8,128)S(1)}, u32[]{:S(2)}, u32[]{:S(2)}) collective-permute-start(f32[3,14,14,4]{3,2,1,0:T(8,128)S(1)} %get-tuple-element.232), channel_id=1, source_target_pairs={{1,0},{2,1},{3,2},{4,3},{5,4},{6,5},{7,6},{9,8},{10,9},{11,10},{12... | collective-permute-start | bytes 28232 | tf_op jit(solution)/shard_map/ppermute | solution.py:45
  323.5 9.3 %collective-permute-start.8 = (f32[20,8,1,128]{3,2,1,0:T(1,128)S(1)}, f32[20,8,1,128]{3,2,1,0:T(1,128)S(1)}, u32[]{:S(2)}, u32[]{:S(2)}) collective-permute-start(f32[20,8,1,128]{3,2,1,0:T(1,128)S(1)} %get-tuple-element.208), channel_id=1, source_target_pairs={{0,8},{8,16},{16,24},{24,32},{32,40},{40,48},{48,56},{1,9},{9,17},... | collective-permute-start | bytes 245768 | tf_op jit(solution)/shard_map/ppermute | solution.py:44
  325.4 7.4 %collective-permute-start.9 = (f32[20,8,1,128]{3,2,1,0:T(1,128)S(1)}, f32[20,8,1,128]{3,2,1,0:T(1,128)S(1)}, u32[]{:S(2)}, u32[]{:S(2)}) collective-permute-start(f32[20,8,1,128]{3,2,1,0:T(1,128)S(1)} %get-tuple-element.209), channel_id=1, source_target_pairs={{8,0},{16,8},{24,16},{32,24},{40,32},{48,40},{56,48},{9,1},{17,9},... | collective-permute-start | bytes 245768 | tf_op jit(solution)/shard_map/ppermute | solution.py:45
  334.4 12.4 %collective-permute-start.11 = (f32[20,8,8,1]{0,2,3,1:T(8,128)S(1)}, f32[20,8,8,1]{0,2,3,1:T(8,128)S(1)}, u32[]{:S(2)}, u32[]{:S(2)}) collective-permute-start(f32[20,8,8,1]{0,2,3,1:T(8,128)S(1)} %copy.206), channel_id=1, source_target_pairs={{1,0},{2,1},{3,2},{4,3},{5,4},{6,5},{7,6},{9,8},{10,9},{11,10},{12... | collective-permute-start | bytes 15368 | tf_op jit(solution)/shard_map/ppermute | solution.py:45
  339.0 7.0 %collective-permute-start.10 = (f32[20,8,8,1]{0,2,3,1:T(8,128)S(1)}, f32[20,8,8,1]{0,2,3,1:T(8,128)S(1)}, u32[]{:S(2)}, u32[]{:S(2)}) collective-permute-start(f32[20,8,8,1]{0,2,3,1:T(8,128)S(1)} %copy.205), channel_id=1, source_target_pairs={{0,1},{1,2},{2,3},{3,4},{4,5},{5,6},{6,7},{8,9},{9,10},{10,11},{11... | collective-permute-start | bytes 15368 | tf_op jit(solution)/shard_map/ppermute | solution.py:44
where the time goes:
time: 352 us; the launch traced here: 350 us
  loops' own time  90.3 us (26%)
  other arithmetic  73.7 us (21%)
  starting transfers between devices  68.8 us (20%)
  matrix products  53.9 us (15%)
  local copies, waits for them, and re-layouts  33.5 us (10%)
  waiting for transfers between devices  28.1 us (8%)
    another operation x1, loops' own time, on_device(): lax.scan(add_neighbour, jnp.zeros((3, block_x, block_y, block_z), jnp.flo...  90.3 us
    dot_general x27, matrix products, spread_block(): jnp.dot(weighted, weight_z.T, precision=lax.Precision.HIGHEST, preferred_...  50.2 us
    ppermute x9, starting transfers between devices, extended_2(): before = lax.ppermute(last, axis, up)  38.9 us
    ppermute x9, starting transfers between devices, extended_2(): after = lax.ppermute(initial, axis, down)  29.9 us
    scatter-add x3, other arithmetic, compute_membrane_force(): vertex_forces.at[:, :, triangles[:, second_corner]].add(-tension)  29 us
    scatter-add x3, other arithmetic, compute_membrane_force(): vertex_forces.at[:, :, triangles[:, first_corner]].add(tension)  28.7 us
    ppermute x9, waiting for transfers between devices, extended_2(): after = lax.ppermute(initial, axis, down)  16.1 us
    dynamic_slice x27, local copies, waits for them, and re-layouts, on_device(): lax.scan(add_neighbour, jnp.zeros((3, block_x, block_y, block_z), jnp.flo...  15.8 us
  transfers between devices with their start and end apart: 18, of which 7 were waited for; matrix products, arithmetic and copies ran while one was open for 2% of the time, Pallas kernels for 0%

commit v1 on v0

v1 whole, which is shorter than its diff:
```python
import functools
import itertools
import math

import jax
import jax.numpy as jnp
from jax import lax
from jax.experimental import pallas as pl
from jax.experimental.pallas import tpu as pltpu
from jax.sharding import PartitionSpec as P

MESH = pl.DeviceIdType.MESH
AXES = ("gx", "gy", "gz")
NV = 642
VP = 768
NT = 1280
BX, BY, BZ = 6, 6, 128
F32, BF16, I32 = jnp.float32, jnp.bfloat16, jnp.int32
FAR = -10000
STIFFNESS, REST, TAU = 0.1, 4.0, 0.8

LATTICE = (
    (0, 0, 0),
    (1, 0, 0),
    (-1, 0, 0),
    (0, 1, 0),
    (0, -1, 0),
    (0, 0, 1),
    (0, 0, -1),
    (1, 1, 0),
    (-1, -1, 0),
    (1, -1, 0),
    (-1, 1, 0),
    (1, 0, 1),
    (-1, 0, -1),
    (1, 0, -1),
    (-1, 0, 1),
    (0, 1, 1),
    (0, -1, -1),
    (0, 1, -1),
    (0, -1, 1),
)
WEIGHT = [1.0 / 3.0] + [1.0 / 18.0] * 6 + [1.0 / 36.0] * 12
NUMBER = {c: q for q, c in enumerate(LATTICE)}

RHO, FLAG, VEL = 19, 20, 21

FACE = {
    (1, 0): ({1: 1, 7: 7, 3: 11, 5: 13, 2: 9}, 0, 4),
    (-1, 0): ({2: 2, 0: 8, 4: 12, 6: 14, 3: 10}, 1, 5),
    (0, 1): ({3: 3, 7: 7, 2: 10, 1: 17, 0: 15}, 4, 5),
    (0, -1): ({4: 4, 0: 8, 1: 9, 2: 18, 3: 16}, 5, 6),
    (1, 1): ({7: 7}, 3, 4),
    (1, -1): ({1: 9}, 3, 4),
    (-1, 1): ({2: 10}, 3, 4),
    (-1, -1): ({0: 8}, 3, 4),
}
TRAVELS = [d for d in itertools.product((-1, 0, 1), repeat=3) if d != (0, 0, 0)]
TRAVELS.sort(key=lambda d: (d[0] == 0, d[2] != 0, d[1] != 0))


def layout():
    where, row = {}, 0
    for d in TRAVELS:
        dx, dy, dz = d
        rows = {}
        rows["F"] = (16 if dz == 0 else 8) * (2 if dx == 0 else 1)
        if dz == 0:
            rows["U"] = 96 if dy == 0 else (72 if dx == 0 else 48)
            rows["R"] = 8 if dx and dy else 48
        elif dx:
            rows["Z"] = 8
        else:
            rows["Z"] = 16 if dy else 64
        spot, begin = {}, row
        for part, count in rows.items():
            spot[part] = row
            row += count
        where[d] = (begin, row - begin, spot)
    return where, row


WHERE, ROWS = layout()


def iota(shape, axis):
    return lax.broadcasted_iota(I32, shape, axis)


def bits(index, members):
    code = sum(1 << m for m in members)
    return (lax.shift_right_logical(jnp.full(index.shape, code, I32), index) & 1) == 1


def per_row(sub, values):
    out = jnp.zeros(sub.shape, F32)
    for value in sorted(set(values)):
        if value != 0:
            members = [r for r, v in enumerate(values) if v == value]
            out = jnp.where(bits(sub, members), F32(value), out)
    return out


def constants(sub, numbers):
    rows = [[0 if q is None else LATTICE[q][a] for q in numbers] for a in range(3)]
    rows.append([0 if q is None else WEIGHT[q] for q in numbers])
    return [per_row(sub, r) for r in rows]


def natural_numbers(k):
    return [q if q < 19 else None for q in range(8 * k, 8 * k + 8)]


def sin_half_pi(f):
    t = f * (0.5 * math.pi)
    t2 = t * t
    out = jnp.full(f.shape, 1.0 / math.factorial(13), F32)
    for k in (11, 9, 7, 5, 3, 1):
        sign = 1.0 if (13 - k) // 2 % 2 == 0 else -1.0
        out = out * t2 + sign / math.factorial(k)
    return out * t


def node_weights(n, base, four):
    d = n - base
    out = jnp.where(d == 3, four[3], 0.0)
    for k in (2, 1, 0):
        out = jnp.where(d == k, four[k], out)
    return out


def four_weights(frac, axis):
    s = sin_half_pi(frac)[axis : axis + 1]
    c = sin_half_pi(1.0 - frac)[axis : axis + 1]
    return [0.25 * (1.0 - s), 0.25 * (1.0 + c), 0.25 * (1.0 + s), 0.25 * (1.0 - c)]


def halves(x):
    hi = x.astype(BF16)
    return hi, (x - hi.astype(F32)).astype(BF16)


def thirds(x):
    hi = x.astype(BF16)
    rest = x - hi.astype(F32)
    mid = rest.astype(BF16)
    return jnp.concatenate([hi, mid, (rest - mid.astype(F32)).astype(BF16)], axis=0)


def dot(a, b, ca, cb):
    return lax.dot_general(a, b, (((ca,), (cb,)), ((), ())), preferred_element_type=F32)


def load_vertices(base, off, base_s, off_s):
    base_s[...] = jnp.full((8, VP), FAR, I32)
    off_s[...] = jnp.zeros((8, VP), F32)
    for a in range(3):
        base_s[a : a + 1, 0:NV] = base[a]
        off_s[a : a + 1, 0:NV] = off[a]


def membrane(base_s, off_s, alive, tri, incidence, mono):
    def fill(step, carry):
        rows = pl.multiple_of(step * 16, 16)
        vertex = iota((16, NT), 0) + rows
        hit = (vertex == tri[0:1]) | (vertex == tri[1:2]) | (vertex == tri[2:3])
        incidence[pl.ds(rows, 16), :] = jnp.where(hit, 1.0, 0.0).astype(BF16)
        return carry

    lax.fori_loop(0, 41, fill, 0)
    incidence[656:VP, :] = jnp.zeros((VP - 656, NT), BF16)
    base = base_s[...]
    real = base > FAR // 2
    low = jnp.min(jnp.where(real, base, 1 << 20), axis=1, keepdims=True)
    at = jnp.where(real, (base - low - 3).astype(F32) + off_s[...], 0.0)
    x = [at[a : a + 1] for a in range(3)]
    r2 = x[0] * x[0] + x[1] * x[1] + x[2] * x[2]
    pairs = ((0, 0), (1, 1), (2, 2), (0, 1), (0, 2), (1, 2))
    rows = [(r2 - REST * REST) * v for v in x] + [x[a] * x[b] for a, b in pairs] + x
    mono[...] = jnp.zeros((16, VP), F32)
    for r, value in enumerate(rows):
        mono[r : r + 1, :] = value
    mono[12:13, :] = jnp.ones((1, VP), F32)
    sums = dot(thirds(mono[...]), incidence[...], 1, 0)
    sums = sums[0:16] + sums[16:32] + sums[32:48]
    back = dot(thirds(sums), incidence[...], 1, 1)
    back = back[0:16] + back[16:32] + back[32:48]
    row = [back[r : r + 1] for r in range(13)]
    xx = {}
    for k, (a, b) in enumerate(pairs):
        xx[a, b] = xx[b, a] = row[3 + k]
    lin, count = row[9:12], row[12]
    along = x[0] * lin[0] + x[1] * lin[1] + x[2] * lin[2]
    trace = xx[0, 0] + xx[1, 1] + xx[2, 2]
    common = 2.0 * along - r2 * count - (trace - REST * REST * count)
    loads = []
    for a in range(3):
        turned = xx[a, 0] * x[0] + xx[a, 1] * x[1] + xx[a, 2] * x[2]
        total = row[a] - 2.0 * turned + r2 * lin[a] + x[a] * common
        loads.append((STIFFNESS / (REST * REST)) * alive * total)
    return loads


YN = {0: (0, 1, 2, 3, 4, 5, 6, -1), 1: (6, 7, 8, 9, 10, 11, 12, 5), -1: (-6, -5, -4, -3, -2, -1, 0, -7)}
DYS = (0, 1, -1)


def spread_own(base_s, off_s, loads, outer, mid):
    base, frac = base_s[...], off_s[...]
    four = [four_weights(frac, a) for a in range(3)]
    real = base[2:3] > FAR // 2
    low = jnp.min(jnp.where(real, base[2:3], 1 << 20), axis=1, keepdims=True)
    k = iota((32, 1), 0)
    z = jnp.where(k < 16, low + k, jnp.where(k < 24, 127 - 16 + k, -7 - 24 + k))
    wz = node_weights(z, base[2:3], four[2])
    left = jnp.concatenate([wz * load for load in loads], axis=0)
    wx = node_weights(iota((16, 1), 0) - 4, base[0:1], four[0])
    row8 = iota((8, 1), 0)
    for i, dy in enumerate(DYS):
        n = jnp.where(row8 == 7, YN[dy][7], row8 + YN[dy][0])
        wy = node_weights(n, base[1:2], four[1])
        for j in range(5):
            outer[i * 128 + j * 8 : i * 128 + j * 8 + 8, :] = wx[9 + j : 10 + j] * wy
            outer[i * 128 + 40 + j * 8 : i * 128 + 48 + j * 8, :] = wx[j : j + 1] * wy
        outer[i * 128 + 80 : i * 128 + 128, :] = jnp.zeros((48, VP), F32)
        for j in range(8):
            mid[i * 64 + j * 8 : i * 64 + j * 8 + 8, :] = wx[3 + j : 4 + j] * wy
    l_hi, l_lo = halves(left)
    both = jnp.concatenate([l_hi, l_lo], axis=0)

    def product(ref):
        r_hi, r_lo = halves(ref[...])
        out = dot(both, r_hi, 1, 1)
        return out[0:96] + out[96:192] + dot(l_hi, r_lo, 1, 1)

    return product(outer), product(mid), z[0:16].astype(F32)


def roll(x, shift, axis):
    shift = shift % x.shape[axis]
    return x if shift == 0 else pltpu.roll(x, shift, axis)


def force_pieces(outer, mid, z16, lane, dx, dy, dz, put):
    k0, kn = {0: (0, 16), 1: (16, 8), -1: (24, 8)}[dz]
    i = DYS.index(dy)
    lane = iota((kn, 128), 1)
    if dx:
        off = 0 if dx == 1 else 40
        out = jnp.zeros((kn, 128), F32)
        for c in range(3):
            tile = outer[32 * c + k0 : 32 * c + k0 + kn, i * 128 : i * 128 + 128]
            tile = roll(tile, 40 * c - off, 1)
            out = jnp.where((lane >= 40 * c) & (lane < 40 * c + 40), tile, out)
        if dz == 0:
            out = jnp.where(lane >= 120, z16, out)
        put(0, out)
        return
    tiles = []
    for c in range(3):
        t = i // 2 * 128
        tile = mid[32 * c + k0 : 32 * c + k0 + kn, t : t + (128 if i < 2 else 64)]
        if i == 2:
            tile = jnp.concatenate([tile, jnp.zeros((kn, 64), F32)], axis=1)
        tiles.append(roll(tile, 64 * (c % 2) - 64 * (i % 2), 1))
    put(0, jnp.where(lane < 64, tiles[0], tiles[1]))
    rest = z16 if dz == 0 else jnp.zeros((kn, 128), F32)
    put(kn, jnp.where(lane < 64, tiles[2], rest))


def pack(tiles, lane):
    out = jnp.zeros((8, 128), F32)
    for s, tile in enumerate(tiles):
        out = jnp.where((lane >= 8 * s) & (lane < 8 * s + 8), roll(tile, 4 + 8 * s, 1), out)
    return out


def unpack(packed, s):
    return roll(packed, -(4 + 8 * (s % 16)), 1)


def coords():
    return [lax.axis_index(a) for a in AXES]


def present(sizes, me, d):
    ok = None
    for m, s, size in zip(me, d, sizes):
        if s:
            here = m < size - 1 if s == 1 else m > 0
            ok = here if ok is None else jnp.logical_and(ok, here)
    return ok


def kernel_a(sizes, pops, mask, base, off, occ, tri, col, vel, ownf, recv, send, base_s, off_s, incidence, mono, outer, mid, vout, rho_s, edge_s, zero, send_sem, recv_sem, zero_sem):
    me = coords()
    barrier = pltpu.get_barrier_semaphore()
    count = jnp.int32(0)
    for d in TRAVELS:
        ok = present(sizes, me, d)
        count = count + ok.astype(I32)

        @pl.when(ok)
        def _():
            there = tuple(m + s for m, s in zip(me, d))
            pl.semaphore_signal(barrier, inc=1, device_id=there, device_id_type=MESH)

    lane = iota((8, 128), 1)
    sub = iota((8, 128), 0)
    zero[...] = jnp.zeros(zero.shape, F32)

    def blank(d):
        begin, rows, _ = WHERE[d]
        return pltpu.make_async_copy(zero.at[pl.ds(0, rows)], recv.at[pl.ds(begin, rows)], zero_sem.at[TRAVELS.index(d)])

    def back(d):
        return tuple(-s for s in d)

    for d in TRAVELS:

        @pl.when(jnp.logical_not(present(sizes, me, back(d))))
        def _():
            blank(d).start()

    cs = [constants(sub, natural_numbers(k)) for k in range(3)]
    vout[...] = jnp.zeros(vout.shape, F32)
    rho_s[...] = jnp.zeros(rho_s.shape, F32)
    flags = mask[...].astype(F32)

    def columns(x, carry):
        for y in range(BY):
            i = x * BY + y
            col[i, 16:24, :] = jnp.zeros((8, 128), F32)
            col[i, 0:19, :] = pops[i]
            v = [col[i, 8 * k : 8 * k + 8, :] for k in range(3)]
            rho = jnp.sum(v[0] + v[1] + v[2], axis=0, keepdims=True)
            col[i, RHO : RHO + 1, :] = rho
            rho_s[x, y : y + 1, :] = rho
            col[i, FLAG : FLAG + 1, :] = mask[x, y : y + 1, :].astype(F32)
            for a in range(3):
                m = v[0] * cs[0][a] + v[1] * cs[1][a] + v[2] * cs[2][a]
                u = jnp.sum(m, axis=0, keepdims=True) / rho
                col[i, VEL + a : VEL + a + 1, :] = u
                vout[a, x, y : y + 1, :] = u
        return carry

    lax.fori_loop(0, BX, columns, 0)
    vel[...] = vout[...]
    for e, (dx, dy) in enumerate(((1, 0), (-1, 0), (0, 1), (0, -1))):
        up, down = NUMBER[dx, dy, 1], NUMBER[dx, dy, -1]
        edge_s[e] = jnp.zeros((24, 128), F32)
        for j in range(6):
            i = (5 if dx == 1 else 0) * BY + j if dx else j * BY + (5 if dy == 1 else 0)
            both = jnp.where(lane[0:1] >= 64, col[i, up : up + 1, :], col[i, down : down + 1, :])
            edge_s[e, j : j + 1, :] = both
            edge_s[e, 8 + j : 9 + j, :] = col[i, RHO : RHO + 1, :]
            edge_s[e, 16 + j : 17 + j, :] = col[i, FLAG : FLAG + 1, :]

    def ring_tile(i, face):
        rows, r_rho, r_flag = FACE[face]
        out = jnp.where(sub == r_rho, col[i, RHO : RHO + 1, :], col[i, FLAG : FLAG + 1, :])
        moves = {}
        for r, q in rows.items():
            moves.setdefault((q // 8, (r - q) % 8), []).append(r)
        for (k, shift), members in moves.items():
            out = jnp.where(bits(sub, members), roll(col[i, 8 * k : 8 * k + 8, :], shift, 0), out)
        return out

    packs = {}
    for e, dx in ((0, 1), (1, -1)):
        xs = range(2, 6) if dx == 1 else range(4)
        tiles = [vout[a, x] for a in range(3) for x in xs]
        tiles += [edge_s[e, 8 * t : 8 * t + 8, :] for t in range(3)]
        packs[dx] = pack(tiles, lane)
    us = [vout[a, x] for a in range(3) for x in range(6)]
    first = pack(us[:16], lane)
    for d in TRAVELS:
        dx, dy, dz = d
        spot = WHERE[d][2]
        if dz:
            z = spot["Z"]
            if dx:
                send[z : z + 8, :] = packs[dx]
            elif dy:
                e = 2 if dy == 1 else 3
                send[z : z + 8, :] = first
                send[z + 8 : z + 16, :] = pack(us[16:] + [edge_s[e, 8 * t : 8 * t + 8, :] for t in range(3)], lane)
            continue
        u, r = spot["U"], spot["R"]
        xs = {0: range(6), 1: range(2, 6), -1: range(4)}[dx]
        if dy == 0:
            for t, (a, x) in enumerate(itertools.product(range(3), xs)):
                send[u + 8 * t : u + 8 * t + 8, :] = vout[a, x]
        else:
            half = len(xs) // 2
            for t, (a, j) in enumerate(itertools.product(range(3), range(half))):
                one, two = vout[a, xs[2 * j]], vout[a, xs[2 * j + 1]]
                if dy == 1:
                    tile = jnp.where(sub >= 4, roll(one, 2, 0), roll(two, 6, 0))
                else:
                    tile = jnp.where(bits(sub, (0, 1, 6, 7)), roll(one, 6, 0), roll(two, 2, 0))
                send[u + 8 * t : u + 8 * t + 8, :] = tile
        if dx and dy:
            i = (5 if dx == 1 else 0) * BY + (5 if dy == 1 else 0)
            send[r : r + 8, :] = ring_tile(i, (dx, dy))
        else:
            for j in range(6):
                i = (5 if dx == 1 else 0) * BY + j if dx else j * BY + (5 if dy == 1 else 0)
                send[r + 8 * j : r + 8 * j + 8, :] = ring_tile(i, (dx, dy))
    for dz in (1, -1):
        z = WHERE[0, 0, dz][2]["Z"]
        if dz == 1:
            for t in range(8):
                tiles = []
                for s in range(16 * t, min(16 * t + 16, 126)):
                    tiles.append(col[s // 3, 8 * (s % 3) : 8 * (s % 3) + 8, :] if s < 108 else us[s - 108])
                send[z + 8 * t : z + 8 * t + 8, :] = pack(tiles, lane)
            done = z
        else:
            send[z : z + 64, :] = send[done : done + 64, :]

    load_vertices(base, off, base_s, off_s)
    alive = (occ[...] > 0).astype(F32)
    loads = membrane(base_s, off_s, alive, tri, incidence, mono)
    f_outer, f_mid, z16 = spread_own(base_s, off_s, loads, outer, mid)

    def own_put(k, tile):
        ownf[k : k + tile.shape[0], :] = tile

    force_pieces(f_outer, f_mid, z16, lane, 0, 0, 0, own_put)
    for d in TRAVELS:

        def put(k, tile, f=WHERE[d][2]["F"]):
            send[f + k : f + k + tile.shape[0], :] = tile

        force_pieces(f_outer, f_mid, z16, lane, *d, put)

    pl.semaphore_wait(barrier, count)

    def message(d):
        begin, rows, _ = WHERE[d]
        t = TRAVELS.index(d)
        return pltpu.make_async_remote_copy(
            src_ref=send.at[pl.ds(begin, rows)],
            dst_ref=recv.at[pl.ds(begin, rows)],
            send_sem=send_sem.at[t],
            recv_sem=recv_sem.at[t],
            device_id=tuple(m + s for m, s in zip(me, d)),
            device_id_type=MESH,
        )

    for d in TRAVELS:

        @pl.when(present(sizes, me, d))
        def _():
            message(d).start()

    for d in TRAVELS:

        @pl.when(present(sizes, me, d))
        def _():
            message(d).wait_send()

        @pl.when(present(sizes, me, back(d)))
        def _():
            message(d).wait_recv()

        @pl.when(jnp.logical_not(present(sizes, me, back(d))))
        def _():
            blank(d).wait()


def collide(p, c, rho, u, f):
    inv = 0.5 / rho
    v = [a + inv * b for a, b in zip(u, f)]
    vv = v[0] * v[0] + v[1] * v[1] + v[2] * v[2]
    vf = v[0] * f[0] + v[1] * f[1] + v[2] * f[2]
    factor = 1.0 - 0.5 / TAU
    a0 = (1.0 / TAU) * rho * (1.0 - 1.5 * vv) - (3.0 * factor) * vf
    a1 = (3.0 / TAU) * rho
    a2 = (4.5 / TAU) * rho
    cx, cy, cz, w = c
    pr = cx * v[0] + cy * v[1] + cz * v[2]
    cf = cx * f[0] + cy * f[1] + cz * f[2]
    poly = a0 + pr * (a1 + a2 * pr) + cf * (3.0 * factor + (9.0 * factor) * pr)
    return (1.0 - 1.0 / TAU) * p + w * poly


def forces(recv, ownf, force):
    zl = iota((1, 256), 1)
    zl = jnp.where(zl < 132, zl, jnp.where(zl >= 252, zl - 256, -5000)).astype(F32)
    k8 = iota((8, 1), 0).astype(F32)
    out = {}
    for sx in (-1, 0, 1):
        parts, zs = [], []
        for sy, sz in itertools.product((-1, 0, 1), (0, -1, 1)):
            kn = 8 if sz else 16
            if (sx, sy, sz) == (0, 0, 0):
                ref, f = ownf, 0
            else:
                ref, f = recv, WHERE[-sx, -sy, -sz][2]["F"]
            tile = ref[f : f + kn, :]
            if sx == 0:
                tile = jnp.concatenate([tile, ref[f + kn : f + 2 * kn, :]], axis=1)
            parts.append(tile)
            if sz == 0:
                zs.append(tile[:, 120:121] if sx else tile[:, 192:193])
            else:
                zs.append(k8 + (-1.0 if sz == -1 else 121.0))
        g = jnp.concatenate(parts, axis=0)
        z = jnp.concatenate(zs, axis=0)
        place = jnp.where(z == zl, 1.0, 0.0).astype(BF16)
        hi, lo = halves(g.T)
        out[sx] = dot(hi, place, 1, 0) + dot(lo, place, 1, 0)
    for a, x in itertools.product(range(3), range(8)):
        tile = out[0][64 * a + 8 * x : 64 * a + 8 * x + 8]
        if x < 5:
            tile = tile + out[-1][40 * a + 8 * x : 40 * a + 8 * x + 8]
        if x >= 3:
            tile = tile + out[1][40 * a + 8 * x - 24 : 40 * a + 8 * x - 16]
        force[a, x] = tile


def assemble(recv, vel, ext, lane, sub):
    low4 = (lane & 7) < 4
    above_rows = bits(sub, (0, 1))
    for sx in (-1, 0, 1):
        xs = range(6) if sx == 0 else range(4)
        x0 = {-1: 0, 0: 4, 1: 10}[sx]
        above, below = WHERE[-sx, -1, 0][2]["U"], WHERE[-sx, 1, 0][2]["U"]
        half = len(xs) // 2
        for a, x in itertools.product(range(3), xs):
            if sx == 0:
                own = vel[a, x]
            else:
                u = WHERE[-sx, 0, 0][2]["U"] + 8 * (a * 4 + x)
                own = recv[u : u + 8, :]
            t = 8 * (a * half + x // 2)
            up = recv[above + t : above + t + 8, :]
            dn = recv[below + t : below + t + 8, :]
            if x % 2:
                up, dn = roll(up, 4, 0), roll(dn, 4, 0)
            ext[a, x0 + x, 0:8, 0:128] = jnp.where(sub < 6, own, up)
            ext[a, x0 + x, 8:16, 0:128] = jnp.where(above_rows, up, jnp.where(sub >= 4, dn, 0.0))

        def merged(sy, t):
            lower = WHERE[-sx, -sy, 1][2]["Z"] + 8 * t
            upper = WHERE[-sx, -sy, -1][2]["Z"] + 8 * t
            return jnp.where(low4, recv[lower : lower + 8, :], recv[upper : upper + 8, :])

        count = 3 * len(xs)
        for t in range((count + 15) // 16):
            if sx == 0:
                slots = range(16 * t, min(16 * t + 16, count))
                m_up, m_dn = merged(1, t), merged(-1, t)
            else:
                slots = range(count)
                m_up, m_dn = merged(1, 0), merged(-1, 0)
            m_up, m_dn = roll(m_up, 6, 0), roll(m_dn, 2, 0)
            second = jnp.where(above_rows, m_up, jnp.where(sub >= 4, m_dn, 0.0))
            for s in slots:
                a, x = s // len(xs), s % len(xs)
                own_slot = s + 108 if sx == 0 else s
                own = unpack(merged(0, own_slot // 16), own_slot)
                ext[a, x0 + x, 0:8, 128:256] = jnp.where(sub < 6, own, unpack(m_up, s))
                ext[a, x0 + x, 8:16, 128:256] = unpack(second, s)


def interpolate(ext, base_s, off_s, occ, wz_s, out):
    base, frac = base_s[...], off_s[...]
    four = [four_weights(frac, a) for a in range(3)]
    wx = node_weights(iota((16, 1), 0) - 4, base[0:1], four[0])
    n = iota((16, 1), 0)
    wy = node_weights(jnp.where(n < 10, n, n - 16), base[1:2], four[1])
    wz_s[...] = jnp.zeros(wz_s.shape, F32)
    wz_s[0:136, :] = node_weights(iota((136, 1), 0), base[2:3], four[2])
    wz_s[248:256, :] = node_weights(iota((8, 1), 0) - 8, base[2:3], four[2])
    w_hi, w_lo = halves(wz_s[...])
    alive = (occ[...] > 0).astype(F32)
    for a in range(3):
        e_hi, e_lo = halves(ext[a].reshape(14 * 16, 256))
        p = dot(e_hi, w_hi, 1, 0) + dot(e_lo, w_hi, 1, 0) + dot(e_hi, w_lo, 1, 0)
        total = jnp.zeros((16, VP), F32)
        for x in range(14):
            total = total + p[16 * x : 16 * x + 16] * wx[x : x + 1]
        row = jnp.sum(total * wy, axis=0, keepdims=True) * alive
        out[a] = row[:, 0:NV]


def kernel_b(col, vel, ownf, recv, base, off, occ, nxt, vtx, base_s, off_s, ext, force, raw, moved, wz_s):
    lane = iota((8, 128), 1)
    sub = iota((8, 128), 0)
    load_vertices(base, off, base_s, off_s)
    forces(recv, ownf, force)
    assemble(recv, vel, ext, lane, sub)
    interpolate(ext, base_s, off_s, occ, wz_s, vtx)

    wall = jnp.full((8, 128), jnp.nan, F32)
    low4 = (lane & 7) < 4
    side = jnp.where(lane[0:1] >= 64, 1.0, -1.0)

    def shifts(cz):
        edge = ((cz > 0.5) & (lane == 127)) | ((cz < -0.5) & (lane == 0))

        def move(s, z):
            a = jnp.where(edge, z, s)
            return jnp.where(cz > 0.5, roll(a, 1, 1), jnp.where(cz < -0.5, roll(a, 127, 1), a))

        return move

    cs = [constants(sub, natural_numbers(k)) for k in range(3)]
    movers = [shifts(c[2]) for c in cs]
    z_low = WHERE[0, 0, 1][2]["Z"]
    z_high = WHERE[0, 0, -1][2]["Z"]
    merged = []
    for t in range(7):
        merged.append(jnp.where(low4, recv[z_low + 8 * t : z_low + 8 * t + 8, :], recv[z_high + 8 * t : z_high + 8 * t + 8, :]))
    for x, y in itertools.product(range(BX), range(BY)):
        i = x * BY + y
        rho, flag = col[i, RHO : RHO + 1, :], col[i, FLAG : FLAG + 1, :]
        u = [col[i, VEL + a : VEL + a + 1, :] for a in range(3)]
        f = [force[a, x + 1, y : y + 1, 0:128] for a in range(3)]
        fz = [force[a, x + 1, y : y + 1, 128:256] for a in range(3)]
        zt = [unpack(merged[(3 * i + k) // 16], 3 * i + k) for k in range(3)]
        uz = [zt[2][VEL - 16 + a : VEL - 15 + a] for a in range(3)]
        rho_z, flag_z = zt[2][RHO - 16 : RHO - 15], zt[2][FLAG - 16 : FLAG - 15]
        for k in range(3):
            r = collide(col[i, 8 * k : 8 * k + 8, :], cs[k], rho, u, f)
            raw[i, 8 * k : 8 * k + 8, :] = r
            rz = collide(zt[k], cs[k], rho_z, uz, fz)
            s = jnp.where(flag > 0.5, r, wall)
            sz = jnp.where(flag_z > 0.5, rz, wall)
            moved[x + 1, y + 1, 8 * k : 8 * k + 8, :] = movers[k](s, sz)

    for face, (rows, r_rho, r_flag) in FACE.items():
        dx, dy = face
        numbers = [rows.get(r) for r in range(8)]
        c = constants(sub, numbers)
        mover = shifts(c[2])
        ring = WHERE[dx, dy, 0][2]["R"]
        count = 1 if dx and dy else 6
        if count == 6:
            if dx:
                z = [WHERE[dx, 0, s][2]["Z"] for s in (1, -1)]
                slot = 12
            else:
                z = [WHERE[0, dy, s][2]["Z"] + 8 for s in (1, -1)]
                slot = 2
            pz = jnp.where(low4, recv[z[0] : z[0] + 8, :], recv[z[1] : z[1] + 8, :])
            tz = [unpack(pz, slot + t) for t in range(3)]
            cz = (float(dx), float(dy), side, 1.0 / 36.0)
        for j in range(count):
            x = {1: -1, -1: 6, 0: j}[dx]
            y = {1: -1, -1: 6, 0: j}[dy]
            t = recv[ring + 8 * j : ring + 8 * j + 8, :]
            rho, flag = t[r_rho : r_rho + 1], t[r_flag : r_flag + 1]
            yu, yf = y % 16, y % 8
            u = [ext[a, x + 4, yu : yu + 1, 0:128] for a in range(3)]
            f = [force[a, x + 1, yf : yf + 1, 0:128] for a in range(3)]
            s = jnp.where(flag > 0.5, collide(t, c, rho, u, f), wall)
            if count == 6:
                uz = [ext[a, x + 4, yu : yu + 1, 128:256] for a in range(3)]
                fz = [force[a, x + 1, yf : yf + 1, 128:256] for a in range(3)]
                rz = collide(tz[0][j : j + 1], cz, tz[1][j : j + 1], uz, fz)
                sz = jnp.where(tz[2][j : j + 1] > 0.5, rz, wall[0:1])
                s = mover(s, sz)
            for k in sorted({q // 8 for q in rows.values()}):
                out = None
                for shift in sorted({(q - r) % 8 for r, q in rows.items() if q // 8 == k}):
                    tile = roll(s, shift, 0)
                    members = [q % 8 for r, q in rows.items() if q // 8 == k and (q - r) % 8 == shift]
                    out = tile if out is None else jnp.where(bits(sub, members), tile, out)
                moved[x + 1, y + 1, 8 * k : 8 * k + 8, :] = out

    odd = (iota((24, 128), 0) & 1) == 1
    start = iota((24, 128), 0) == 0
    for x, y in itertools.product(range(BX), range(BY)):
        i = x * BY + y
        r = raw[i]
        turned = jnp.where(start, r, jnp.where(odd, roll(r, 23, 0), roll(r, 1, 0)))
        for k in range(3):
            sources = {}
            for q in natural_numbers(k):
                if q is not None:
                    sources.setdefault(LATTICE[q][:2], []).append(q % 8)
            out = None
            for (cx, cy), members in sources.items():
                tile = moved[x + 1 - cx, y + 1 - cy, 8 * k : 8 * k + 8, :]
                out = tile if out is None else jnp.where(bits(sub, members), tile, out)
            out = jnp.where(out == out, out, turned[8 * k : 8 * k + 8])
            last = min(8 * k + 8, 19)
            nxt[i, 8 * k : last, :] = out[0 : last - 8 * k]


def on_device(sizes, populations, fluid_mask, stencil_base, offsets, occupied_cell_slots, triangles):
    pops = jnp.transpose(populations, (1, 2, 0, 3)).reshape(BX * BY, 19, BZ)
    base = stencil_base.reshape(3, 1, NV)
    off = offsets.reshape(3, 1, NV)
    occ = occupied_cell_slots.reshape(1, 1)
    vmem = pl.BlockSpec(memory_space=pltpu.VMEM)
    anywhere = pl.BlockSpec(memory_space=pl.ANY)
    shape = jax.ShapeDtypeStruct
    col, vel, ownf, recv = pl.pallas_call(
        functools.partial(kernel_a, sizes),
        name="load_and_send",
        out_shape=(shape((36, 24, 128), F32), shape((3, 6, 8, 128), F32), shape((32, 128), F32), shape((ROWS, 128), F32)),
        in_specs=[vmem] * 6,
        out_specs=(vmem, vmem, vmem, anywhere),
        scratch_shapes=[
            pltpu.VMEM((ROWS, 128), F32),
            pltpu.VMEM((8, VP), I32),
            pltpu.VMEM((8, VP), F32),
            pltpu.VMEM((VP, NT), BF16),
            pltpu.VMEM((16, VP), F32),
            pltpu.VMEM((384, VP), F32),
            pltpu.VMEM((192, VP), F32),
            pltpu.VMEM((3, 6, 8, 128), F32),
            pltpu.VMEM((6, 8, 128), F32),
            pltpu.VMEM((4, 24, 128), F32),
            pltpu.VMEM((160, 128), F32),
            pltpu.SemaphoreType.DMA((26,)),
            pltpu.SemaphoreType.DMA((26,)),
            pltpu.SemaphoreType.DMA((26,)),
        ],
        compiler_params=pltpu.CompilerParams(collective_id=0, has_side_effects=True, vmem_limit_bytes=48 << 20),
    )(pops, fluid_mask, base, off, occ, triangles.T)
    nxt, vtx = pl.pallas_call(
        kernel_b,
        name="collide_and_pass",
        out_shape=(shape((36, 19, 128), F32), shape((3, 1, NV), F32)),
        in_specs=[vmem] * 7,
        out_specs=(vmem, vmem),
        scratch_shapes=[
            pltpu.VMEM((8, VP), I32),
            pltpu.VMEM((8, VP), F32),
            pltpu.VMEM((3, 14, 16, 256), F32),
            pltpu.VMEM((3, 8, 8, 256), F32),
            pltpu.VMEM((36, 24, 128), F32),
            pltpu.VMEM((8, 8, 24, 128), F32),
            pltpu.VMEM((256, VP), F32),
        ],
        compiler_params=pltpu.CompilerParams(vmem_limit_bytes=48 << 20),
    )(col, vel, ownf, recv, base, off, occ)
    nxt = jnp.transpose(nxt.reshape(BX, BY, 19, BZ), (2, 0, 1, 3))
    return nxt, vtx.reshape(1, 1, 1, 3, NV)


def solution(mesh):
    sizes = tuple(mesh.shape[a] for a in AXES)
    placed = (
        P(None, "gx", "gy", "gz"),
        P("gx", "gy", "gz"),
        P("gx", "gy", "gz", None, None),
        P("gx", "gy", "gz", None, None),
        P("gx", "gy", "gz"),
        P(),
    )
    return jax.shard_map(
        functools.partial(on_device, sizes),
        mesh=mesh,
        in_specs=placed,
        out_specs=(P(None, "gx", "gy", "gz"), P("gx", "gy", "gz", None, None)),
        check_vma=False,
    )
```

time: 352 us -> 36.7 us (0.10)
  the two profiles are of different devices: /device:TPU:206 before, /device:TPU:63 now
where the time goes in v1:
time: 36.7 us; the launch traced here: 36.3 us
  Pallas kernels  31.8 us (87%)
  local copies, waits for them, and re-layouts  3.21 us (9%)
  between operations  1.31 us (4%)
    pallas_call x1, Pallas kernels, on_device(): pl.pallas_call(functools.partial(kernel_a, sizes), name='load_and_send',...  28.1 us
    pallas_call x1, Pallas kernels, on_device(): pl.pallas_call(kernel_b, name='collide_and_pass', out_shape=(shape((36, 1...  3.66 us
    unnamed x10, local copies, waits for them, and re-layouts  3.21 us

profile of v1, /device:TPU:63, one launch (start us, length us, event | category | flops | bytes accessed | tf_op | source)
XLA Modules:
  0.0 36.3 jit_solution(10982072379144340160)
XLA Ops:
  0.6 0.0 copy-start.1
  1.3 0.0 copy-done.1
  1.3 0.0 copy-start
  1.3 1.0 %copy-done = f32[19,6,6,128]{3,0,2,1:T(8,128)S(1)} copy-done((f32[19,6,6,128]{3,0,2,1:T(8,128)S(1)}, f32[19,6,6,128]{3,0,2,1:T(8,128)}, u32[]{:S(2)}) %copy-start) | copy-done | bytes 350232
  2.3 0.0 copy-start.2
  2.3 0.7 %copy-done.2 = f32[1,1,1,3,642]{4,2,3,1,0:T(1,128)S(1)} copy-done((f32[1,1,1,3,642]{4,2,3,1,0:T(1,128)S(1)}, f32[1,1,1,3,642]{4,2,3,1,0:T(1,128)}, u32[]{:S(2)}) %copy-start.2) | copy-done | bytes 7728
  3.0 0.0 copy-start.3
  3.0 0.7 %copy-done.3 = s32[6,6,128]{2,1,0:T(8,128)S(1)} copy-done((s32[6,6,128]{2,1,0:T(8,128)S(1)}, s32[6,6,128]{2,1,0:T(8,128)}, u32[]{:S(2)}) %copy-start.3) | copy-done | bytes 18456
  3.8 0.0 copy-start.4
  3.8 0.7 %copy-done.4 = s32[1280,3]{0,1:T(4,128)S(1)} copy-done((s32[1280,3]{0,1:T(4,128)S(1)}, s32[1280,3]{0,1:T(4,128)}, u32[]{:S(2)}) %copy-start.4) | copy-done | bytes 15384
  4.5 28.1 %load_and_send.1 = (f32[36,24,128]{2,1,0:T(8,128)S(1)}, f32[3,6,8,128]{3,2,1,0:T(8,128)S(1)}, f32[32,128]{1,0:T(8,128)S(1)}, f32[1392,128]{1,0:T(8,128)S(1)}) custom-call(f32[36,19,128]{2,1,0:T(8,128)S(1)} %bitcast.15, s32[6,6,128]{2,1,0:T(8,128)S(1)} %copy-done.3, s32[3,1,642]{2,1,0:T(1,128)S(1)} %bitcast.16, f32[3,1,642]{2,1,0:T(1,128)S(1)} %bitcast.18, ...), custom_call_target="tpu_custom_call" | custom-call | tf_op jit(solution)/shard_map/load_and_send/pallas_call | solution.py:703
  32.7 3.7 %collide_and_pass.1 = (f32[36,19,128]{2,1,0:T(8,128)}, f32[3,1,642]{2,1,0:T(1,128)}) custom-call(f32[36,24,128]{2,1,0:T(8,128)S(1)} %get-tuple-element.8.col, f32[3,6,8,128]{3,2,1,0:T(8,128)S(1)} %get-tuple-element.9.vel, f32[32,128]{1,0:T(8,128)S(1)} %get-tuple-element.10.ownf, f32[1392,128]{1,0:T(8,128)S(1)} %get-tuple-element.11.recv, ...), custom_call_target="tpu_custom_call" | custom-call | tf_op jit(solution)/shard_map/collide_and_pass/pallas_call | solution.py:727
Async XLA Ops:
  0.6 0.7 %copy-start.1 = (s32[1,1,1,3,642]{4,2,3,1,0:T(1,128)S(1)}, s32[1,1,1,3,642]{4,2,3,1,0:T(1,128)}, u32[]{:S(2)}) copy-start(s32[1,1,1,3,642]{4,2,3,1,0:T(1,128)} %param.8) | copy-start | bytes 23116
  1.3 1.0 %copy-start = (f32[19,6,6,128]{3,0,2,1:T(8,128)S(1)}, f32[19,6,6,128]{3,0,2,1:T(8,128)}, u32[]{:S(2)}) copy-start(f32[19,6,6,128]{3,0,2,1:T(8,128)} %param.6) | copy-start | bytes 1050628
  2.3 0.7 %copy-start.2 = (f32[1,1,1,3,642]{4,2,3,1,0:T(1,128)S(1)}, f32[1,1,1,3,642]{4,2,3,1,0:T(1,128)}, u32[]{:S(2)}) copy-start(f32[1,1,1,3,642]{4,2,3,1,0:T(1,128)} %param.9) | copy-start | bytes 23116
  3.0 0.7 %copy-start.3 = (s32[6,6,128]{2,1,0:T(8,128)S(1)}, s32[6,6,128]{2,1,0:T(8,128)}, u32[]{:S(2)}) copy-start(s32[6,6,128]{2,1,0:T(8,128)} %mask.1) | copy-start | bytes 55300
  3.8 0.7 %copy-start.4 = (s32[1280,3]{0,1:T(4,128)S(1)}, s32[1280,3]{0,1:T(4,128)}, u32[]{:S(2)}) copy-start(s32[1280,3]{0,1:T(4,128)} %param.11) | copy-start | bytes 46084

commit v2 on v1

--- a/solution.py
+++ b/solution.py
@@ -50,10 +50,10 @@
     (-1, 0): ({2: 2, 0: 8, 4: 12, 6: 14, 3: 10}, 1, 5),
     (0, 1): ({3: 3, 7: 7, 2: 10, 1: 17, 0: 15}, 4, 5),
     (0, -1): ({4: 4, 0: 8, 1: 9, 2: 18, 3: 16}, 5, 6),
-    (1, 1): ({7: 7}, 3, 4),
-    (1, -1): ({1: 9}, 3, 4),
-    (-1, 1): ({2: 10}, 3, 4),
-    (-1, -1): ({0: 8}, 3, 4),
+    (1, 1): ({7: 7}, 0, 4),
+    (1, -1): ({2: 9}, 0, 4),
+    (-1, 1): ({3: 10}, 1, 5),
+    (-1, -1): ({0: 8}, 1, 5),
 }
 TRAVELS = [d for d in itertools.product((-1, 0, 1), repeat=3) if d != (0, 0, 0)]
 TRAVELS.sort(key=lambda d: (d[0] == 0, d[2] != 0, d[1] != 0))
@@ -66,7 +66,7 @@
         rows = {}
         rows["F"] = (16 if dz == 0 else 8) * (2 if dx == 0 else 1)
         if dz == 0:
-            rows["U"] = 96 if dy == 0 else (72 if dx == 0 else 48)
+            rows["U"] = 48 if dx and dy else 72
             rows["R"] = 8 if dx and dy else 48
         elif dx:
             rows["Z"] = 8
@@ -81,6 +81,7 @@
 
 
 WHERE, ROWS = layout()
+XROWS = {1: 0, -1: 120}
 
 
 def iota(shape, axis):
@@ -283,7 +284,7 @@
     return [lax.axis_index(a) for a in AXES]
 
 
-def present(sizes, me, d):
+def present_at(sizes, me, d):
     ok = None
     for m, s, size in zip(me, d, sizes):
         if s:
@@ -292,8 +293,44 @@
     return ok
 
 
-def kernel_a(sizes, pops, mask, base, off, occ, tri, col, vel, ownf, recv, send, base_s, off_s, incidence, mono, outer, mid, vout, rho_s, edge_s, zero, send_sem, recv_sem, zero_sem):
+def face_tiles(ref, begin, sub):
+    tiles = []
+    for a in range(3):
+        t = [ref[begin + 8 * (3 * a + j) : begin + 8 * (3 * a + j) + 8, :] for j in range(3)]
+        last = jnp.where(sub < 2, roll(t[0], 2, 0), jnp.where(sub < 4, roll(t[1], 4, 0), roll(t[2], 6, 0)))
+        tiles += t + [last]
+    return tiles
+
+
+def paired(tiles, half, dy, sub):
+    out = []
+    for t in range(3 * half):
+        one, two = tiles[2 * t], tiles[2 * t + 1]
+        if dy == 1:
+            out.append(jnp.where(sub >= 4, roll(one, 2, 0), roll(two, 6, 0)))
+        else:
+            out.append(jnp.where(bits(sub, (0, 1, 6, 7)), roll(one, 6, 0), roll(two, 2, 0)))
+    return out
+
+
+def back(d):
+    return tuple(-s for s in d)
+
+
+def kernel_a(sizes, pops, mask, base, off, occ, tri, col, vel, ownf, base_s, off_s, recvx, recv, send, passed, mask_s, base_v, off_v, tri_v, incidence, mono, outer, mid, edge_s, zero, in_sem, send_sem, recv_sem, fsend_sem, frecv_sem, zero_sem):
     me = coords()
+    there = {d: present_at(sizes, me, d) for d in TRAVELS}
+
+    def present(sizes, me, d):
+        return there[d]
+
+    ins = [(pops, col.at[:, pl.ds(0, 19), :]), (mask, mask_s), (base, base_v), (off, off_v), (tri, tri_v)]
+    ins = [pltpu.make_async_copy(a, b, in_sem.at[k]) for k, (a, b) in enumerate(ins)]
+    for copy in ins:
+        copy.start()
+    def at(d):
+        return tuple(m + s for m, s in zip(me, d))
+
     barrier = pltpu.get_barrier_semaphore()
     count = jnp.int32(0)
     for d in TRAVELS:
@@ -302,8 +339,7 @@
 
         @pl.when(ok)
         def _():
-            there = tuple(m + s for m, s in zip(me, d))
-            pl.semaphore_signal(barrier, inc=1, device_id=there, device_id_type=MESH)
+            pl.semaphore_signal(barrier, inc=1, device_id=at(d), device_id_type=MESH)
 
     lane = iota((8, 128), 1)
     sub = iota((8, 128), 0)
@@ -313,48 +349,39 @@
         begin, rows, _ = WHERE[d]
         return pltpu.make_async_copy(zero.at[pl.ds(0, rows)], recv.at[pl.ds(begin, rows)], zero_sem.at[TRAVELS.index(d)])
 
-    def back(d):
-        return tuple(-s for s in d)
-
     for d in TRAVELS:
 
         @pl.when(jnp.logical_not(present(sizes, me, back(d))))
         def _():
             blank(d).start()
 
+    for dx in (1, -1):
+
+        @pl.when(jnp.logical_not(present(sizes, me, (-dx, 0, 0))))
+        def _():
+            recvx[XROWS[dx] : XROWS[dx] + 120, :] = jnp.zeros((120, 128), F32)
+
     cs = [constants(sub, natural_numbers(k)) for k in range(3)]
-    vout[...] = jnp.zeros(vout.shape, F32)
-    rho_s[...] = jnp.zeros(rho_s.shape, F32)
-    flags = mask[...].astype(F32)
+    vel[...] = jnp.zeros(vel.shape, F32)
+    for copy in ins:
+        copy.wait()
 
     def columns(x, carry):
         for y in range(BY):
             i = x * BY + y
-            col[i, 16:24, :] = jnp.zeros((8, 128), F32)
-            col[i, 0:19, :] = pops[i]
+            col[i, 19:24, :] = jnp.zeros((5, 128), F32)
             v = [col[i, 8 * k : 8 * k + 8, :] for k in range(3)]
             rho = jnp.sum(v[0] + v[1] + v[2], axis=0, keepdims=True)
             col[i, RHO : RHO + 1, :] = rho
-            rho_s[x, y : y + 1, :] = rho
-            col[i, FLAG : FLAG + 1, :] = mask[x, y : y + 1, :].astype(F32)
+            col[i, FLAG : FLAG + 1, :] = mask_s[x, y : y + 1, :].astype(F32)
             for a in range(3):
                 m = v[0] * cs[0][a] + v[1] * cs[1][a] + v[2] * cs[2][a]
                 u = jnp.sum(m, axis=0, keepdims=True) / rho
                 col[i, VEL + a : VEL + a + 1, :] = u
-                vout[a, x, y : y + 1, :] = u
+                vel[a, x, y : y + 1, :] = u
         return carry
 
     lax.fori_loop(0, BX, columns, 0)
-    vel[...] = vout[...]
-    for e, (dx, dy) in enumerate(((1, 0), (-1, 0), (0, 1), (0, -1))):
-        up, down = NUMBER[dx, dy, 1], NUMBER[dx, dy, -1]
-        edge_s[e] = jnp.zeros((24, 128), F32)
-        for j in range(6):
-            i = (5 if dx == 1 else 0) * BY + j if dx else j * BY + (5 if dy == 1 else 0)
-            both = jnp.where(lane[0:1] >= 64, col[i, up : up + 1, :], col[i, down : down + 1, :])
-            edge_s[e, j : j + 1, :] = both
-            edge_s[e, 8 + j : 9 + j, :] = col[i, RHO : RHO + 1, :]
-            edge_s[e, 16 + j : 17 + j, :] = col[i, FLAG : FLAG + 1, :]
 
     def ring_tile(i, face):
         rows, r_rho, r_flag = FACE[face]
@@ -366,62 +393,94 @@
             out = jnp.where(bits(sub, members), roll(col[i, 8 * k : 8 * k + 8, :], shift, 0), out)
         return out
 
-    packs = {}
-    for e, dx in ((0, 1), (1, -1)):
+    for dx in (1, -1):
+        u, r = WHERE[dx, 0, 0][2]["U"], WHERE[dx, 0, 0][2]["R"]
         xs = range(2, 6) if dx == 1 else range(4)
-        tiles = [vout[a, x] for a in range(3) for x in xs]
-        tiles += [edge_s[e, 8 * t : 8 * t + 8, :] for t in range(3)]
-        packs[dx] = pack(tiles, lane)
-    us = [vout[a, x] for a in range(3) for x in range(6)]
+        for a, j in itertools.product(range(3), range(3)):
+            t = u + 8 * (3 * a + j)
+            send[t : t + 8, :] = jnp.where(sub < 6, vel[a, xs[j]], roll(vel[a, xs[3]], 6 - 2 * j, 0))
+        for y in range(6):
+            send[r + 8 * y : r + 8 * y + 8, :] = ring_tile((5 if dx == 1 else 0) * BY + y, (dx, 0))
+    us = [vel[a, x] for a in range(3) for x in range(6)]
     first = pack(us[:16], lane)
-    for d in TRAVELS:
+    for dy in (1, -1):
+        u, r = WHERE[0, dy, 0][2]["U"], WHERE[0, dy, 0][2]["R"]
+        for t, tile in enumerate(paired(us, 3, dy, sub)):
+            send[u + 8 * t : u + 8 * t + 8, :] = tile
+        up, down = NUMBER[0, dy, 1], NUMBER[0, dy, -1]
+        edge_s[...] = jnp.zeros((24, 128), F32)
+        for x in range(6):
+            i = x * BY + (5 if dy == 1 else 0)
+            send[r + 8 * x : r + 8 * x + 8, :] = ring_tile(i, (0, dy))
+            edge_s[x : x + 1, :] = jnp.where(lane[0:1] >= 64, col[i, up : up + 1, :], col[i, down : down + 1, :])
+            edge_s[8 + x : 9 + x, :] = col[i, RHO : RHO + 1, :]
+            edge_s[16 + x : 17 + x, :] = col[i, FLAG : FLAG + 1, :]
+        second = pack(us[16:] + [edge_s[8 * t : 8 * t + 8, :] for t in range(3)], lane)
+        for dz in (1, -1):
+            z = WHERE[0, dy, dz][2]["Z"]
+            send[z : z + 8, :] = first
+            send[z + 8 : z + 16, :] = second
+    z = WHERE[0, 0, 1][2]["Z"]
+    for t in range(8):
+        tiles = []
+        for s in range(16 * t, min(16 * t + 16, 126)):
+            tiles.append(col[s // 3, 8 * (s % 3) : 8 * (s % 3) + 8, :] if s < 108 else us[s - 108])
+        send[z + 8 * t : z + 8 * t + 8, :] = pack(tiles, lane)
+
+    pl.semaphore_wait(barrier, count)
+
+    def fields(d):
         dx, dy, dz = d
-        spot = WHERE[d][2]
-        if dz:
-            z = spot["Z"]
-            if dx:
-                send[z : z + 8, :] = packs[dx]
-            elif dy:
-                e = 2 if dy == 1 else 3
-                send[z : z + 8, :] = first
-                send[z + 8 : z + 16, :] = pack(us[16:] + [edge_s[e, 8 * t : 8 * t + 8, :] for t in range(3)], lane)
-            continue
-        u, r = spot["U"], spot["R"]
-        xs = {0: range(6), 1: range(2, 6), -1: range(4)}[dx]
-        if dy == 0:
-            for t, (a, x) in enumerate(itertools.product(range(3), xs)):
-                send[u + 8 * t : u + 8 * t + 8, :] = vout[a, x]
-        else:
-            half = len(xs) // 2
-            for t, (a, j) in enumerate(itertools.product(range(3), range(half))):
-                one, two = vout[a, xs[2 * j]], vout[a, xs[2 * j + 1]]
-                if dy == 1:
-                    tile = jnp.where(sub >= 4, roll(one, 2, 0), roll(two, 6, 0))
-                else:
-                    tile = jnp.where(bits(sub, (0, 1, 6, 7)), roll(one, 6, 0), roll(two, 2, 0))
-                send[u + 8 * t : u + 8 * t + 8, :] = tile
-        if dx and dy:
-            i = (5 if dx == 1 else 0) * BY + (5 if dy == 1 else 0)
-            send[r : r + 8, :] = ring_tile(i, (dx, dy))
-        else:
-            for j in range(6):
-                i = (5 if dx == 1 else 0) * BY + j if dx else j * BY + (5 if dy == 1 else 0)
-                send[r + 8 * j : r + 8 * j + 8, :] = ring_tile(i, (dx, dy))
-    for dz in (1, -1):
-        z = WHERE[0, 0, dz][2]["Z"]
-        if dz == 1:
-            for t in range(8):
-                tiles = []
-                for s in range(16 * t, min(16 * t + 16, 126)):
-                    tiles.append(col[s // 3, 8 * (s % 3) : 8 * (s % 3) + 8, :] if s < 108 else us[s - 108])
-                send[z + 8 * t : z + 8 * t + 8, :] = pack(tiles, lane)
-            done = z
-        else:
-            send[z : z + 64, :] = send[done : done + 64, :]
-
-    load_vertices(base, off, base_s, off_s)
+        begin, rows, spot = WHERE[d]
+        first_row = spot["Z"] if dz else spot["U"]
+        rows = begin + rows - first_row
+        src, dst = send.at[pl.ds(first_row, rows)], recv.at[pl.ds(first_row, rows)]
+        if dy == 0 and dz == 0:
+            dst = recvx.at[pl.ds(XROWS[dx], rows)]
+        elif dx and dz:
+            src = passed.at[pl.ds(0 if dx == 1 else 8, rows)]
+        elif dx == 0 and dy == 0:
+            src = send.at[pl.ds(z, rows)]
+        step = (0, dy, dz) if dx and (dy or dz) else d
+        t = TRAVELS.index(d)
+        return pltpu.make_async_remote_copy(
+            src_ref=src,
+            dst_ref=dst,
+            send_sem=send_sem.at[t],
+            recv_sem=recv_sem.at[t],
+            device_id=at(step),
+            device_id_type=MESH,
+        )
+
+    def force(d):
+        f = WHERE[d][2]["F"]
+        rows = (16 if d[2] == 0 else 8) * (2 if d[0] == 0 else 1)
+        t = TRAVELS.index(d)
+        return pltpu.make_async_remote_copy(
+            src_ref=send.at[pl.ds(f, rows)],
+            dst_ref=recv.at[pl.ds(f, rows)],
+            send_sem=fsend_sem.at[t],
+            recv_sem=frecv_sem.at[t],
+            device_id=at(d),
+            device_id_type=MESH,
+        )
+
+    def sends(d):
+        if d[0] and (d[1] or d[2]):
+            return present(sizes, me, (-d[0], d[1], d[2]))
+        return present(sizes, me, d)
+
+    direct = [d for d in TRAVELS if not (d[0] and (d[1] or d[2]))]
+    relayed = [d for d in TRAVELS if d[0] and (d[1] or d[2])]
+    for d in direct:
+
+        @pl.when(sends(d))
+        def _():
+            fields(d).start()
+
+    load_vertices(base_v, off_v, base_s, off_s)
     alive = (occ[...] > 0).astype(F32)
-    loads = membrane(base_s, off_s, alive, tri, incidence, mono)
+    loads = membrane(base_s, off_s, alive, tri_v, incidence, mono)
     f_outer, f_mid, z16 = spread_own(base_s, off_s, loads, outer, mid)
 
     def own_put(k, tile):
@@ -434,36 +493,64 @@
             send[f + k : f + k + tile.shape[0], :] = tile
 
         force_pieces(f_outer, f_mid, z16, lane, *d, put)
-
-    pl.semaphore_wait(barrier, count)
-
-    def message(d):
-        begin, rows, _ = WHERE[d]
-        t = TRAVELS.index(d)
-        return pltpu.make_async_remote_copy(
-            src_ref=send.at[pl.ds(begin, rows)],
-            dst_ref=recv.at[pl.ds(begin, rows)],
-            send_sem=send_sem.at[t],
-            recv_sem=recv_sem.at[t],
-            device_id=tuple(m + s for m, s in zip(me, d)),
-            device_id_type=MESH,
-        )
-
     for d in TRAVELS:
 
         @pl.when(present(sizes, me, d))
         def _():
-            message(d).start()
+            force(d).start()
+
+    for dx in (-1, 1):
+        got = present(sizes, me, (-dx, 0, 0))
+
+        @pl.when(got)
+        def _():
+            fields((dx, 0, 0)).wait_recv()
+
+        tiles = face_tiles(recvx, XROWS[dx], sub)
+        rows, r_rho, r_flag = FACE[dx, 0]
+        ring = XROWS[dx] + 72
+        row_of = {q: r for r, q in rows.items()}
+        up, down = row_of[NUMBER[dx, 0, 1]], row_of[NUMBER[dx, 0, -1]]
+        edge_s[...] = jnp.zeros((24, 128), F32)
+        for y in range(6):
+            t = recvx[ring + 8 * y : ring + 8 * y + 8, :]
+            edge_s[y : y + 1, :] = jnp.where(lane[0:1] >= 64, t[up : up + 1], t[down : down + 1])
+            edge_s[8 + y : 9 + y, :] = t[r_rho : r_rho + 1]
+            edge_s[16 + y : 17 + y, :] = t[r_flag : r_flag + 1]
+        p = 0 if dx == 1 else 8
+        passed[p : p + 8, :] = pack(tiles + [edge_s[8 * t : 8 * t + 8, :] for t in range(3)], lane)
+        for dy in (1, -1):
+            u, r = WHERE[dx, dy, 0][2]["U"], WHERE[dx, dy, 0][2]["R"]
+            for t, tile in enumerate(paired(tiles, 2, dy, sub)):
+                send[u + 8 * t : u + 8 * t + 8, :] = tile
+            corner = ring + (40 if dy == 1 else 0)
+            send[r : r + 8, :] = recvx[corner : corner + 8, :]
+        for d in relayed:
+            if d[0] == dx:
+
+                @pl.when(sends(d))
+                def _():
+                    fields(d).start()
 
     for d in TRAVELS:
 
+        @pl.when(sends(d))
+        def _():
+            fields(d).wait_send()
+
         @pl.when(present(sizes, me, d))
         def _():
-            message(d).wait_send()
+            force(d).wait_send()
 
         @pl.when(present(sizes, me, back(d)))
         def _():
-            message(d).wait_recv()
+            force(d).wait_recv()
+
+        if d[1] or d[2]:
+
+            @pl.when(present(sizes, me, back(d)))
+            def _():
+                fields(d).wait_recv()
 
         @pl.when(jnp.logical_not(present(sizes, me, back(d))))
         def _():
@@ -521,7 +608,7 @@
         force[a, x] = tile
 
 
-def assemble(recv, vel, ext, lane, sub):
+def assemble(recv, recvx, vel, ext, lane, sub):
     low4 = (lane & 7) < 4
     above_rows = bits(sub, (0, 1))
     for sx in (-1, 0, 1):
@@ -529,12 +616,9 @@
         x0 = {-1: 0, 0: 4, 1: 10}[sx]
         above, below = WHERE[-sx, -1, 0][2]["U"], WHERE[-sx, 1, 0][2]["U"]
         half = len(xs) // 2
+        side = face_tiles(recvx, XROWS[-sx], sub) if sx else None
         for a, x in itertools.product(range(3), xs):
-            if sx == 0:
-                own = vel[a, x]
-            else:
-                u = WHERE[-sx, 0, 0][2]["U"] + 8 * (a * 4 + x)
-                own = recv[u : u + 8, :]
+            own = side[4 * a + x] if sx else vel[a, x]
             t = 8 * (a * half + x // 2)
             up = recv[above + t : above + t + 8, :]
             dn = recv[below + t : below + t + 8, :]
@@ -587,12 +671,11 @@
         out[a] = row[:, 0:NV]
 
 
-def kernel_b(col, vel, ownf, recv, base, off, occ, nxt, vtx, base_s, off_s, ext, force, raw, moved, wz_s):
+def kernel_b(col, vel, ownf, base_s, off_s, recvx, recv, occ, nxt, vtx, ext, force, raw, moved, wz_s):
     lane = iota((8, 128), 1)
     sub = iota((8, 128), 0)
-    load_vertices(base, off, base_s, off_s)
     forces(recv, ownf, force)
-    assemble(recv, vel, ext, lane, sub)
+    assemble(recv, recvx, vel, ext, lane, sub)
     interpolate(ext, base_s, off_s, occ, wz_s, vtx)
 
     wall = jnp.full((8, 128), jnp.nan, F32)
@@ -637,7 +720,8 @@
         numbers = [rows.get(r) for r in range(8)]
         c = constants(sub, numbers)
         mover = shifts(c[2])
-        ring = WHERE[dx, dy, 0][2]["R"]
+        ring = WHERE[dx, dy, 0][2]["R"] if dy else XROWS[dx] + 72
+        ring_ref = recv if dy else recvx
         count = 1 if dx and dy else 6
         if count == 6:
             if dx:
@@ -652,7 +736,7 @@
         for j in range(count):
             x = {1: -1, -1: 6, 0: j}[dx]
             y = {1: -1, -1: 6, 0: j}[dy]
-            t = recv[ring + 8 * j : ring + 8 * j + 8, :]
+            t = ring_ref[ring + 8 * j : ring + 8 * j + 8, :]
             rho, flag = t[r_rho : r_rho + 1], t[r_flag : r_flag + 1]
             yu, yf = y % 16, y % 8
             u = [ext[a, x + 4, yu : yu + 1, 0:128] for a in range(3)]
@@ -698,41 +782,52 @@
     off = offsets.reshape(3, 1, NV)
     occ = occupied_cell_slots.reshape(1, 1)
     vmem = pl.BlockSpec(memory_space=pltpu.VMEM)
-    anywhere = pl.BlockSpec(memory_space=pl.ANY)
+    hbm = pl.BlockSpec(memory_space=pltpu.HBM)
     shape = jax.ShapeDtypeStruct
-    col, vel, ownf, recv = pl.pallas_call(
+    dma = pltpu.SemaphoreType.DMA
+    col, vel, ownf, base_p, off_p, recvx, recv = pl.pallas_call(
         functools.partial(kernel_a, sizes),
         name="load_and_send",
-        out_shape=(shape((36, 24, 128), F32), shape((3, 6, 8, 128), F32), shape((32, 128), F32), shape((ROWS, 128), F32)),
-        in_specs=[vmem] * 6,
-        out_specs=(vmem, vmem, vmem, anywhere),
+        out_shape=(
+            shape((36, 24, 128), F32),
+            shape((3, 6, 8, 128), F32),
+            shape((32, 128), F32),
+            shape((8, VP), I32),
+            shape((8, VP), F32),
+            shape((240, 128), F32),
+            shape((ROWS, 128), F32),
+        ),
+        in_specs=[hbm, hbm, hbm, hbm, vmem, hbm],
+        out_specs=(vmem,) * 6 + (hbm,),
         scratch_shapes=[
             pltpu.VMEM((ROWS, 128), F32),
-            pltpu.VMEM((8, VP), I32),
-            pltpu.VMEM((8, VP), F32),
+            pltpu.VMEM((16, 128), F32),
+            pltpu.VMEM((6, 6, 128), I32),
+            pltpu.VMEM((3, 1, NV), I32),
+            pltpu.VMEM((3, 1, NV), F32),
+            pltpu.VMEM((3, NT), I32),
             pltpu.VMEM((VP, NT), BF16),
             pltpu.VMEM((16, VP), F32),
             pltpu.VMEM((384, VP), F32),
             pltpu.VMEM((192, VP), F32),
-            pltpu.VMEM((3, 6, 8, 128), F32),
-            pltpu.VMEM((6, 8, 128), F32),
-            pltpu.VMEM((4, 24, 128), F32),
-            pltpu.VMEM((160, 128), F32),
-            pltpu.SemaphoreType.DMA((26,)),
-            pltpu.SemaphoreType.DMA((26,)),
-            pltpu.SemaphoreType.DMA((26,)),
+            pltpu.VMEM((24, 128), F32),
+            pltpu.VMEM((152, 128), F32),
+            dma((5,)),
+            dma((26,)),
+            dma((26,)),
+            dma((26,)),
+            dma((26,)),
+            dma((26,)),
         ],
         compiler_params=pltpu.CompilerParams(collective_id=0, has_side_effects=True, vmem_limit_bytes=48 << 20),
-    )(pops, fluid_mask, base, off, occ, triangles.T)
+    )(*(pltpu.with_memory_space_constraint(a, pltpu.HBM) for a in (pops, fluid_mask, base, off)), occ, pltpu.with_memory_space_constraint(triangles.T, pltpu.HBM))
     nxt, vtx = pl.pallas_call(
         kernel_b,
         name="collide_and_pass",
         out_shape=(shape((36, 19, 128), F32), shape((3, 1, NV), F32)),
-        in_specs=[vmem] * 7,
+        in_specs=[vmem] * 8,
         out_specs=(vmem, vmem),
         scratch_shapes=[
-            pltpu.VMEM((8, VP), I32),
-            pltpu.VMEM((8, VP), F32),
             pltpu.VMEM((3, 14, 16, 256), F32),
             pltpu.VMEM((3, 8, 8, 256), F32),
             pltpu.VMEM((36, 24, 128), F32),
@@ -740,7 +835,7 @@
             pltpu.VMEM((256, VP), F32),
         ],
         compiler_params=pltpu.CompilerParams(vmem_limit_bytes=48 << 20),
-    )(col, vel, ownf, recv, base, off, occ)
+    )(col, vel, ownf, base_p, off_p, recvx, recv, occ)
     nxt = jnp.transpose(nxt.reshape(BX, BY, 19, BZ), (2, 0, 1, 3))
     return nxt, vtx.reshape(1, 1, 1, 3, NV)
 

time: 36.7 us -> 31.1 us (0.85)
  the two profiles are of different devices: /device:TPU:63 before, /device:TPU:47 now
where the time goes in v2:
time: 31.1 us; the launch traced here: 30.9 us
  Pallas kernels  29.7 us (95%)
  between operations  1.29 us (4%)
    pallas_call x1, Pallas kernels, on_device(): pl.pallas_call(functools.partial(kernel_a, sizes), name='load_and_send',...  26 us
    pallas_call x1, Pallas kernels, on_device(): pl.pallas_call(kernel_b, name='collide_and_pass', out_shape=(shape((36, 1...  3.63 us

profile of v2, /device:TPU:47, one launch (start us, length us, event | category | flops | bytes accessed | tf_op | source)
XLA Modules:
  0.0 30.9 jit_solution(18266572257909438619)
XLA Ops:
  1.3 26.0 %load_and_send.1 = (f32[36,24,128]{2,1,0:T(8,128)S(1)}, f32[3,6,8,128]{3,2,1,0:T(8,128)S(1)}, f32[32,128]{1,0:T(8,128)S(1)}, s32[8,768]{1,0:T(8,128)S(1)}, f32[8...) custom-call(f32[36,19,128]{2,1,0:T(8,128)} %bitcast.15, s32[6,6,128]{2,1,0:T(8,128)} %mask.1, ...), custom_call_target="tpu_custom_call" | custom-call | tf_op jit(solution)/shard_map/load_and_send/pallas_call | solution.py:788
  27.3 3.6 %collide_and_pass.1 = (f32[36,19,128]{2,1,0:T(8,128)}, f32[3,1,642]{2,1,0:T(1,128)}) custom-call(f32[36,24,128]{2,1,0:T(8,128)S(1)} %get-tuple-element.11.col, f32[3,6,8,128]{3,2,1,0:T(8,128)S(1)} %get-tuple-element.12.vel, f32[32,128]{1,0:T(8,128)S(1)} %get-tuple-element.13.ownf, s32[8,768]{1,0:T(8,128)S(1)} %get-tuple-element.14.base_s, ...), custom_call_target="tpu_custom_call" | custom-call | tf_op jit(solution)/shard_map/collide_and_pass/pallas_call | solution.py:824

commit v3 on v2

v3 whole, which is shorter than its diff:
```python
import functools
import itertools
import math

import jax
import jax.numpy as jnp
from jax import lax
from jax.experimental import pallas as pl
from jax.experimental.pallas import tpu as pltpu
from jax.sharding import PartitionSpec as P

MESH = pl.DeviceIdType.MESH
AXES = ("gx", "gy", "gz")
NV = 642
VP = 768
NT = 1280
BX, BY, BZ = 6, 6, 128
F32, BF16, I32 = jnp.float32, jnp.bfloat16, jnp.int32
FAR = -10000
STIFFNESS, REST, TAU = 0.1, 4.0, 0.8

LATTICE = (
    (0, 0, 0),
    (1, 0, 0),
    (-1, 0, 0),
    (0, 1, 0),
    (0, -1, 0),
    (0, 0, 1),
    (0, 0, -1),
    (1, 1, 0),
    (-1, -1, 0),
    (1, -1, 0),
    (-1, 1, 0),
    (1, 0, 1),
    (-1, 0, -1),
    (1, 0, -1),
    (-1, 0, 1),
    (0, 1, 1),
    (0, -1, -1),
    (0, 1, -1),
    (0, -1, 1),
)
WEIGHT = [1.0 / 3.0] + [1.0 / 18.0] * 6 + [1.0 / 36.0] * 12
NUMBER = {c: q for q, c in enumerate(LATTICE)}

RHO, FLAG, VEL = 19, 20, 21

FACE = {
    (1, 0): ({1: 1, 7: 7, 3: 11, 5: 13, 2: 9}, 0, 4),
    (-1, 0): ({2: 2, 0: 8, 4: 12, 6: 14, 3: 10}, 1, 5),
    (0, 1): ({3: 3, 7: 7, 2: 10, 1: 17, 0: 15}, 4, 5),
    (0, -1): ({4: 4, 0: 8, 1: 9, 2: 18, 3: 16}, 5, 6),
    (1, 1): ({7: 7}, 0, 1),
    (1, -1): ({1: 9}, 0, 2),
    (-1, 1): ({2: 10}, 0, 1),
    (-1, -1): ({0: 8}, 1, 2),
}
UP = {5: 5, 3: 11, 6: 14, 7: 15, 2: 18}
DOWN = {6: 6, 4: 12, 5: 13, 0: 16, 1: 17}
EDGE_VEL = 3
TRAVELS = [d for d in itertools.product((-1, 0, 1), repeat=3) if d != (0, 0, 0)]
TRAVELS.sort(key=lambda d: (d[0] == 0, d[2] != 0, d[1] != 0))


def layout():
    where, row = {}, 0
    for d in TRAVELS:
        dx, dy, dz = d
        rows = {}
        rows["F"] = (16 if dz == 0 else 8) * (2 if dx == 0 else 1)
        if dz == 0:
            rows["R"] = 8 if dx and dy else 48
            rows["U"] = 48 if dx and dy else 72
        elif dx:
            rows["Z"] = 8
        else:
            rows["Z"] = 16 if dy else 40
        spot, begin = {}, row
        for part, count in rows.items():
            spot[part] = row
            row += count
        where[d] = (begin, row - begin, spot)
    return where, row


WHERE, ROWS = layout()


def iota(shape, axis):
    return lax.broadcasted_iota(I32, shape, axis)


def bits(index, members):
    code = sum(1 << m for m in members)
    return (lax.shift_right_logical(jnp.full(index.shape, code, I32), index) & 1) == 1


def per_row(sub, values):
    out = jnp.zeros(sub.shape, F32)
    for value in sorted(set(values)):
        if value != 0:
            members = [r for r, v in enumerate(values) if v == value]
            out = jnp.where(bits(sub, members), F32(value), out)
    return out


def constants(sub, numbers):
    rows = [[0 if q is None else LATTICE[q][a] for q in numbers] for a in range(3)]
    rows.append([0 if q is None else WEIGHT[q] for q in numbers])
    return [per_row(sub, r) for r in rows]


def natural_numbers(k):
    return [q if q < 19 else None for q in range(8 * k, 8 * k + 8)]


def sin_half_pi(f):
    t = f * (0.5 * math.pi)
    t2 = t * t
    out = jnp.full(f.shape, 1.0 / math.factorial(13), F32)
    for k in (11, 9, 7, 5, 3, 1):
        sign = 1.0 if (13 - k) // 2 % 2 == 0 else -1.0
        out = out * t2 + sign / math.factorial(k)
    return out * t


def node_weights(n, base, four):
    d = n - base
    out = jnp.where(d == 3, four[3], 0.0)
    for k in (2, 1, 0):
        out = jnp.where(d == k, four[k], out)
    return out


def four_weights(frac, axis):
    s = sin_half_pi(frac)[axis : axis + 1]
    c = sin_half_pi(1.0 - frac)[axis : axis + 1]
    return [0.25 * (1.0 - s), 0.25 * (1.0 + c), 0.25 * (1.0 + s), 0.25 * (1.0 - c)]


def halves(x):
    hi = x.astype(BF16)
    return hi, (x - hi.astype(F32)).astype(BF16)


def thirds(x):
    hi = x.astype(BF16)
    rest = x - hi.astype(F32)
    mid = rest.astype(BF16)
    return jnp.concatenate([hi, mid, (rest - mid.astype(F32)).astype(BF16)], axis=0)


def dot(a, b, ca, cb):
    return lax.dot_general(a, b, (((ca,), (cb,)), ((), ())), preferred_element_type=F32)


def load_vertices(base, off, base_s, off_s):
    base_s[...] = jnp.full((8, VP), FAR, I32)
    off_s[...] = jnp.zeros((8, VP), F32)
    for a in range(3):
        base_s[a : a + 1, 0:NV] = base[a]
        off_s[a : a + 1, 0:NV] = off[a]


def turn(t, sub):
    one = jnp.where(sub == 2, roll(t, 2, 0), roll(t, 7, 0))
    two = jnp.where(sub == 0, roll(t, 6, 0), roll(t, 1, 0))
    return one, two


def incidence_of(tri, incidence):
    def fill(step, carry):
        rows = pl.multiple_of(step * 16, 16)
        vertex = iota((16, NT), 0) + rows
        hit = (vertex == tri[0:1]) | (vertex == tri[1:2]) | (vertex == tri[2:3])
        incidence[pl.ds(rows, 16), :] = jnp.where(hit, 1.0, 0.0).astype(BF16)
        return carry

    lax.fori_loop(0, 41, fill, 0)
    incidence[656:VP, :] = jnp.zeros((VP - 656, NT), BF16)


def membrane(base_s, off_s, alive, incidence):
    sub = iota((8, VP), 0)
    base = base_s[...]
    x = jnp.where((base > FAR // 2) & (sub < 3), (base - base[:, 0:1]).astype(F32) + off_s[...], 0.0)
    x1, x2 = turn(x, sub)
    xx = x * x
    r2 = xx + x1 * x1 + x2 * x2
    first = (r2 - REST * REST) * x + jnp.where(sub == 3, 1.0, 0.0) + roll(x, 4, 0)
    second = xx + roll(x * x1, 4, 0)
    sums = dot(thirds(jnp.concatenate([first, second], axis=0)), incidence[...], 1, 0)
    sums = sums[0:16] + sums[16:32] + sums[32:48]
    back = dot(thirds(sums), incidence[...], 1, 1)
    back = back[0:16] + back[16:32] + back[32:48]
    cubic, diag = back[0:8], back[8:16]
    count = cubic[3:4]
    lin, cross = roll(cubic, 4, 0), roll(diag, 4, 0)
    turned = diag * x + cross * x1 + turn(cross, sub)[1] * x2
    along, trace = x * lin, jnp.where(sub < 3, diag, 0.0)
    along = along + sum(turn(along, sub))
    trace = trace + sum(turn(trace, sub))
    common = 2.0 * along - r2 * count - (trace - REST * REST * count)
    total = cubic - 2.0 * turned + r2 * lin + x * common
    return (STIFFNESS / (REST * REST)) * alive * total


YN = {0: (0, 1, 2, 3, 4, 5, 6, -1), 1: (6, 7, 8, 9, 10, 11, 12, 5), -1: (-6, -5, -4, -3, -2, -1, 0, -7)}
DYS = (0, 1, -1)


def spread_own(base_s, off_s, loads, outer, mid):
    base, frac = base_s[...], off_s[...]
    four = [four_weights(frac, a) for a in range(3)]
    low = base[2:3, 0:1] - 6
    k = iota((32, 1), 0)
    z = jnp.where(k < 16, low + k, jnp.where(k < 24, 127 - 16 + k, -7 - 24 + k))
    wz = node_weights(z, base[2:3], four[2])
    left = jnp.concatenate([wz * loads[c : c + 1] for c in range(3)], axis=0)
    wx = node_weights(iota((16, 1), 0) - 4, base[0:1], four[0])
    row8 = iota((8, 1), 0)
    for i, dy in enumerate(DYS):
        n = jnp.where(row8 == 7, YN[dy][7], row8 + YN[dy][0])
        wy = node_weights(n, base[1:2], four[1])
        for j in range(5):
            outer[i * 128 + j * 8 : i * 128 + j * 8 + 8, :] = wx[9 + j : 10 + j] * wy
            outer[i * 128 + 40 + j * 8 : i * 128 + 48 + j * 8, :] = wx[j : j + 1] * wy
        outer[i * 128 + 80 : i * 128 + 128, :] = jnp.zeros((48, VP), F32)
        for j in range(8):
            mid[i * 64 + j * 8 : i * 64 + j * 8 + 8, :] = wx[3 + j : 4 + j] * wy
    l_hi, l_lo = halves(left)
    both = jnp.concatenate([l_hi, l_lo], axis=0)

    def product(ref):
        r_hi, r_lo = halves(ref[...])
        out = dot(both, r_hi, 1, 1)
        return out[0:96] + out[96:192] + dot(l_hi, r_lo, 1, 1)

    return product(outer), product(mid), z[0:16].astype(F32)


def roll(x, shift, axis):
    shift = shift % x.shape[axis]
    return x if shift == 0 else pltpu.roll(x, shift, axis)


def force_pieces(outer, mid, z16, lane, dx, dy, dz, put):
    k0, kn = {0: (0, 16), 1: (16, 8), -1: (24, 8)}[dz]
    i = DYS.index(dy)
    lane = iota((kn, 128), 1)
    if dx:
        off = 0 if dx == 1 else 40
        out = jnp.zeros((kn, 128), F32)
        for c in range(3):
            tile = outer[32 * c + k0 : 32 * c + k0 + kn, i * 128 : i * 128 + 128]
            tile = roll(tile, 40 * c - off, 1)
            out = jnp.where((lane >= 40 * c) & (lane < 40 * c + 40), tile, out)
        if dz == 0:
            out = jnp.where(lane >= 120, z16, out)
        put(0, out)
        return
    tiles = []
    for c in range(3):
        t = i // 2 * 128
        tile = mid[32 * c + k0 : 32 * c + k0 + kn, t : t + (128 if i < 2 else 64)]
        if i == 2:
            tile = jnp.concatenate([tile, jnp.zeros((kn, 64), F32)], axis=1)
        tiles.append(roll(tile, 64 * (c % 2) - 64 * (i % 2), 1))
    put(0, jnp.where(lane < 64, tiles[0], tiles[1]))
    rest = z16 if dz == 0 else jnp.zeros((kn, 128), F32)
    put(kn, jnp.where(lane < 64, tiles[2], rest))


def pack(tiles, lane):
    out = jnp.zeros((8, 128), F32)
    for s, tile in enumerate(tiles):
        out = jnp.where((lane >= 8 * s) & (lane < 8 * s + 8), roll(tile, 4 + 8 * s, 1), out)
    return out


def unpack(packed, s):
    return roll(packed, -(4 + 8 * (s % 16)), 1)


def coords():
    return [lax.axis_index(a) for a in AXES]


def present_at(sizes, me, d):
    ok = None
    for m, s, size in zip(me, d, sizes):
        if s:
            here = m < size - 1 if s == 1 else m > 0
            ok = here if ok is None else jnp.logical_and(ok, here)
    return ok


def face_tiles(ref, begin, sub):
    tiles = []
    for a in range(3):
        t = [ref[begin + 8 * (3 * a + j) : begin + 8 * (3 * a + j) + 8, :] for j in range(3)]
        last = jnp.where(sub < 2, roll(t[0], 2, 0), jnp.where(sub < 4, roll(t[1], 4, 0), roll(t[2], 6, 0)))
        tiles += t + [last]
    return tiles


def paired(tiles, half, dy, sub):
    out = []
    for t in range(3 * half):
        one, two = tiles[2 * t], tiles[2 * t + 1]
        if dy == 1:
            out.append(jnp.where(sub >= 4, roll(one, 2, 0), roll(two, 6, 0)))
        else:
            out.append(jnp.where(bits(sub, (0, 1, 6, 7)), roll(one, 6, 0), roll(two, 2, 0)))
    return out


def back(d):
    return tuple(-s for s in d)


def send_all(sizes, pops, mask, base, off, occ, tri, col, vel, ownf, recv, wxy, w_hi, w_lo, send, mask_s, base_v, off_v, tri_v, base_s, off_s, incidence, outer, mid, edge_s, rho_s, in_sem, send_sem, recv_sem, fsend_sem, frecv_sem):
    me = coords()
    there = {d: present_at(sizes, me, d) for d in TRAVELS}

    def present(sizes, me, d):
        return there[d]

    ins = [(pops, col.at[:, pl.ds(0, 19), :]), (mask, mask_s.at[:, pl.ds(0, 6), :]), (base, base_v), (off, off_v), (tri, tri_v)]
    ins = [pltpu.make_async_copy(a, b, in_sem.at[k]) for k, (a, b) in enumerate(ins)]
    for copy in ins:
        copy.start()
    def at(d):
        return tuple(m + s for m, s in zip(me, d))

    barrier = pltpu.get_barrier_semaphore()
    count = jnp.int32(0)
    for d in TRAVELS:
        ok = present(sizes, me, d)
        count = count + ok.astype(I32)

        @pl.when(ok)
        def _():
            pl.semaphore_signal(barrier, inc=1, device_id=at(d), device_id_type=MESH)

    lane = iota((8, 128), 1)
    sub = iota((8, 128), 0)
    for d in TRAVELS:

        @pl.when(jnp.logical_not(present(sizes, me, back(d))))
        def _():
            begin, rows, _ = WHERE[d]
            recv[begin : begin + rows, :] = jnp.zeros((rows, 128), F32)

    cs = [constants(sub, natural_numbers(k)) for k in range(3)]
    vel[...] = jnp.zeros(vel.shape, F32)
    rho_s[...] = jnp.zeros(rho_s.shape, F32)
    for copy in ins:
        copy.wait()

    def columns(x, carry):
        for y in range(BY):
            i = x * BY + y
            col[i, 19:24, :] = jnp.zeros((5, 128), F32)
            v = [col[i, 8 * k : 8 * k + 8, :] for k in range(3)]
            rho = jnp.sum(v[0] + v[1] + v[2], axis=0, keepdims=True)
            col[i, RHO : RHO + 1, :] = rho
            rho_s[x, y : y + 1, :] = rho
            col[i, FLAG : FLAG + 1, :] = mask_s[x, y : y + 1, :].astype(F32)
            for a in range(3):
                m = v[0] * cs[0][a] + v[1] * cs[1][a] + v[2] * cs[2][a]
                u = jnp.sum(m, axis=0, keepdims=True) / rho
                col[i, VEL + a : VEL + a + 1, :] = u
                vel[a, x, y : y + 1, :] = u
        return carry

    lax.fori_loop(0, BX, columns, 0)

    def ring_tile(i, face):
        rows, r_rho, r_flag = FACE[face]
        out = jnp.where(sub == r_rho, col[i, RHO : RHO + 1, :], col[i, FLAG : FLAG + 1, :])
        moves = {}
        for r, q in rows.items():
            moves.setdefault((q // 8, (r - q) % 8), []).append(r)
        for (k, shift), members in moves.items():
            out = jnp.where(bits(sub, members), roll(col[i, 8 * k : 8 * k + 8, :], shift, 0), out)
        return out

    def ends_of(e_rows, dx, dy, column):
        up, down = NUMBER[dx, dy, 1], NUMBER[dx, dy, -1]
        edge_s[...] = jnp.zeros((24, 128), F32)
        for j in range(6):
            i = column(j)
            edge_s[j : j + 1, :] = jnp.where(lane[0:1] >= 64, col[i, up : up + 1, :], col[i, down : down + 1, :])
            edge_s[8 + j : 9 + j, :] = col[i, RHO : RHO + 1, :]
            edge_s[16 + j : 17 + j, :] = col[i, FLAG : FLAG + 1, :]
        return [edge_s[8 * t : 8 * t + 8, :] for t in range(3)]

    us = [vel[a, x] for a in range(3) for x in range(6)]
    first = pack(us[:16], lane)
    for dx in (1, -1):
        u, r = WHERE[dx, 0, 0][2]["U"], WHERE[dx, 0, 0][2]["R"]
        xs = range(2, 6) if dx == 1 else range(4)
        x = 5 if dx == 1 else 0
        for a, j in itertools.product(range(3), range(3)):
            t = u + 8 * (3 * a + j)
            send[t : t + 8, :] = jnp.where(sub < 6, vel[a, xs[j]], roll(vel[a, xs[3]], 6 - 2 * j, 0))
        for y in range(6):
            send[r + 8 * y : r + 8 * y + 8, :] = ring_tile(x * BY + y, (dx, 0))
        tiles = [vel[a, k] for a in range(3) for k in xs] + ends_of(edge_s, dx, 0, lambda j: x * BY + j)
        packed = pack(tiles, lane)
        for dy, dz in itertools.product((0, 1, -1), (1, -1)):
            z = WHERE[dx, dy, dz][2]["Z"]
            send[z : z + 8, :] = packed
        for dy in (1, -1):
            r = WHERE[dx, dy, 0][2]["R"]
            i = x * BY + (5 if dy == 1 else 0)
            send[r : r + 8, :] = ring_tile(i, (dx, dy))
            send[r + EDGE_VEL : r + EDGE_VEL + 3, :] = col[i, VEL : VEL + 3, :]
            u = WHERE[dx, dy, 0][2]["U"]
            for t, tile in enumerate(paired(tiles, 2, dy, sub)):
                send[u + 8 * t : u + 8 * t + 8, :] = tile
    for dy in (1, -1):
        u, r = WHERE[0, dy, 0][2]["U"], WHERE[0, dy, 0][2]["R"]
        y = 5 if dy == 1 else 0
        for t, tile in enumerate(paired(us, 3, dy, sub)):
            send[u + 8 * t : u + 8 * t + 8, :] = tile
        for x in range(6):
            send[r + 8 * x : r + 8 * x + 8, :] = ring_tile(x * BY + y, (0, dy))
        second = pack(us[16:] + ends_of(edge_s, 0, dy, lambda j: j * BY + y), lane)
        for dz in (1, -1):
            z = WHERE[0, dy, dz][2]["Z"]
            send[z : z + 8, :] = first
            send[z + 8 : z + 16, :] = second
    z = WHERE[0, 0, 1][2]["Z"]
    pick = []
    for k in range(2):
        ups = [r for r, q in UP.items() if q // 8 == k]
        downs = [r for r, q in DOWN.items() if q // 8 == k]
        pick.append(((lane >= 64) & bits(sub, ups)) | ((lane < 64) & bits(sub, downs)))
    tiles = []
    for i in range(BX * BY):
        v = [col[i, 8 * k : 8 * k + 8, :] for k in range(3)]
        tiles.append(jnp.where(pick[0], v[0], jnp.where(pick[1], v[1], v[2])))
    tiles += [rho_s[x] for x in range(6)] + [mask_s[x].astype(F32) for x in range(6)] + us
    for t in range(5):
        send[z + 8 * t : z + 8 * t + 8, :] = pack(tiles[16 * t : 16 * t + 16], lane)

    load_vertices(base_v, off_v, base_s, off_s)
    alive = (occ[...] > 0).astype(F32)
    incidence_of(tri_v, incidence)
    pl.semaphore_wait(barrier, count)

    def copy(src, dst, rows, to, sems, t):
        return pltpu.make_async_remote_copy(
            src_ref=send.at[pl.ds(src, rows)],
            dst_ref=recv.at[pl.ds(dst, rows)],
            send_sem=sems[0].at[t],
            recv_sem=sems[1].at[t],
            device_id=at(to),
            device_id_type=MESH,
        )

    faces = [d for d in TRAVELS if sum(map(abs, d)) == 1]
    edges = [d for d in TRAVELS if d[0] and d[1] and d[2] == 0]

    early = faces + edges

    def fields(d):
        begin, rows, spot = WHERE[d]
        row = spot["Z"] if d[2] else spot["U"] if d in edges else spot["R"]
        src = WHERE[0, 0, 1][2]["Z"] if d[2] else row
        return copy(src, row, begin + rows - row, d, (send_sem, recv_sem), TRAVELS.index(d))

    def force_copy(d):
        begin, rows, spot = WHERE[d]
        if d in faces:
            rows = spot["Z" if d[2] else "R"] - begin
        elif d in edges:
            rows = 24
        return copy(begin, begin, rows, d, (fsend_sem, frecv_sem), TRAVELS.index(d))

    for d in early:

        @pl.when(present(sizes, me, d))
        def _():
            fields(d).start()

    loads = membrane(base_s, off_s, alive, incidence)
    f_outer, f_mid, z16 = spread_own(base_s, off_s, loads, outer, mid)

    def own_put(k, tile):
        ownf[k : k + tile.shape[0], :] = tile

    force_pieces(f_outer, f_mid, z16, lane, 0, 0, 0, own_put)
    for d in TRAVELS:

        def put(k, tile, f=WHERE[d][2]["F"]):
            send[f + k : f + k + tile.shape[0], :] = tile

        force_pieces(f_outer, f_mid, z16, lane, *d, put)
    for d in TRAVELS:

        @pl.when(present(sizes, me, d))
        def _():
            force_copy(d).start()

    prepare(base_s, off_s, wxy, w_hi, w_lo)

    for d in TRAVELS:

        @pl.when(present(sizes, me, back(d)))
        def _():
            force_copy(d).wait_recv()
            if d in early:
                fields(d).wait_recv()

    for d in TRAVELS:

        @pl.when(present(sizes, me, d))
        def _():
            force_copy(d).wait_send()
            if d in early:
                fields(d).wait_send()


def collide(p, c, rho, u, f):
    inv = 0.5 / rho
    v = [a + inv * b for a, b in zip(u, f)]
    vv = v[0] * v[0] + v[1] * v[1] + v[2] * v[2]
    vf = v[0] * f[0] + v[1] * f[1] + v[2] * f[2]
    factor = 1.0 - 0.5 / TAU
    a0 = (1.0 / TAU) * rho * (1.0 - 1.5 * vv) - (3.0 * factor) * vf
    a1 = (3.0 / TAU) * rho
    a2 = (4.5 / TAU) * rho
    cx, cy, cz, w = c
    pr = cx * v[0] + cy * v[1] + cz * v[2]
    cf = cx * f[0] + cy * f[1] + cz * f[2]
    poly = a0 + pr * (a1 + a2 * pr) + cf * (3.0 * factor + (9.0 * factor) * pr)
    return (1.0 - 1.0 / TAU) * p + w * poly


def forces(recv, ownf, force):
    zl = iota((1, 256), 1)
    zl = jnp.where(zl < 132, zl, jnp.where(zl >= 252, zl - 256, -5000)).astype(F32)
    k8 = iota((8, 1), 0).astype(F32)
    out = {}
    for sx in (-1, 0, 1):
        parts, zs = [], []
        for sy, sz in itertools.product((-1, 0, 1), (0, -1, 1)):
            kn = 8 if sz else 16
            if (sx, sy, sz) == (0, 0, 0):
                ref, f = ownf, 0
            else:
                ref, f = recv, WHERE[-sx, -sy, -sz][2]["F"]
            tile = ref[f : f + kn, :]
            if sx == 0:
                tile = jnp.concatenate([tile, ref[f + kn : f + 2 * kn, :]], axis=1)
            parts.append(tile)
            if sz == 0:
                zs.append(tile[:, 120:121] if sx else tile[:, 192:193])
            else:
                zs.append(k8 + (-1.0 if sz == -1 else 121.0))
        g = jnp.concatenate(parts, axis=0)
        z = jnp.concatenate(zs, axis=0)
        place = jnp.where(z == zl, 1.0, 0.0).astype(BF16)
        hi, lo = halves(g.T)
        out[sx] = dot(hi, place, 1, 0) + dot(lo, place, 1, 0)
    for a, x in itertools.product(range(3), range(8)):
        tile = out[0][64 * a + 8 * x : 64 * a + 8 * x + 8]
        if x < 5:
            tile = tile + out[-1][40 * a + 8 * x : 40 * a + 8 * x + 8]
        if x >= 3:
            tile = tile + out[1][40 * a + 8 * x - 24 : 40 * a + 8 * x - 16]
        force[a, x] = tile


SIDES = (-1, 0, 1)
X0 = {-1: 0, 0: 4, 1: 10}


def spans(sx):
    return range(6) if sx == 0 else range(4)


def assemble(recv, vel, ext, lane, sub):
    low4 = (lane & 7) < 4
    above_rows = bits(sub, (0, 1))
    for sx in SIDES:
        xs = spans(sx)
        side = face_tiles(recv, WHERE[-sx, 0, 0][2]["U"], sub) if sx else None
        above, below = WHERE[-sx, -1, 0][2]["U"], WHERE[-sx, 1, 0][2]["U"]
        for a, x in itertools.product(range(3), xs):
            own = side[4 * a + x] if sx else vel[a, x]
            t = 8 * (a * (len(xs) // 2) + x // 2)
            up = recv[above + t : above + t + 8, :]
            dn = recv[below + t : below + t + 8, :]
            if x % 2:
                up, dn = roll(up, 4, 0), roll(dn, 4, 0)
            ext[a, X0[sx] + x, 0:8, 0:128] = jnp.where(sub < 6, own, up)
            ext[a, X0[sx] + x, 8:16, 0:128] = jnp.where(above_rows, up, jnp.where(sub >= 4, dn, 0.0))

        def merged(sy, t):
            lower = WHERE[-sx, -sy, 1][2]["Z"] + 8 * t
            upper = WHERE[-sx, -sy, -1][2]["Z"] + 8 * t
            return jnp.where(low4, recv[lower : lower + 8, :], recv[upper : upper + 8, :])

        count = 3 * len(xs)
        for t in range((count + 15) // 16):
            slots = range(16 * t, min(16 * t + 16, count))
            m_up, m_dn = roll(merged(1, t), 6, 0), roll(merged(-1, t), 2, 0)
            m_own = merged(0, t + 3 if sx == 0 else t)
            inner = jnp.where(sub < 6, m_own, m_up)
            second = jnp.where(above_rows, m_up, jnp.where(sub >= 4, m_dn, 0.0))
            for s in slots:
                a, x = s // len(xs), s % len(xs)
                ext[a, X0[sx] + x, 0:8, 128:256] = unpack(inner, s)
                ext[a, X0[sx] + x, 8:16, 128:256] = unpack(second, s)


def prepare(base_s, off_s, wxy, w_hi, w_lo):
    base, frac = base_s[...], off_s[...]
    four = [four_weights(frac, a) for a in range(3)]
    n = iota((16, 1), 0)
    wxy[0:16, :] = node_weights(n - 4, base[0:1], four[0])
    wxy[16:32, :] = node_weights(jnp.where(n < 10, n, n - 16), base[1:2], four[1])
    w_hi[...] = jnp.zeros(w_hi.shape, BF16)
    w_lo[...] = jnp.zeros(w_lo.shape, BF16)
    for begin, rows, shift in ((0, 144, 0), (240, 16, 256)):
        hi, lo = halves(node_weights(iota((rows, 1), 0) + (begin - shift), base[2:3], four[2]))
        w_hi[begin : begin + rows, :] = hi
        w_lo[begin : begin + rows, :] = lo


def interpolate(ext, wxy, w_hi, w_lo, alive, out):
    wy = wxy[16:32, :]
    for a in range(3):
        e_hi, e_lo = halves(ext[a].reshape(14 * 16, 256))
        p = dot(e_hi, w_hi[...], 1, 0) + dot(e_lo, w_hi[...], 1, 0) + dot(e_hi, w_lo[...], 1, 0)
        total = jnp.zeros((16, VP), F32)
        for x in range(14):
            total = total + p[16 * x : 16 * x + 16] * wxy[x : x + 1, :]
        row = jnp.sum(total * wy, axis=0, keepdims=True) * alive
        out[a] = row[:, 0:NV]


def step_nodes(col, recv, ext, force, raw, moved, ends, nxt, lane, sub):
    wall = jnp.full((8, 128), jnp.nan, F32)
    low4 = (lane & 7) < 4
    side = jnp.where(lane[0:1] >= 64, 1.0, -1.0)

    def shifts(cz):
        edge = ((cz > 0.5) & (lane == 127)) | ((cz < -0.5) & (lane == 0))

        def move(s, z):
            a = jnp.where(edge, z, s)
            return jnp.where(cz > 0.5, roll(a, 1, 1), jnp.where(cz < -0.5, roll(a, 127, 1), a))

        return move

    cs = [constants(sub, natural_numbers(k)) for k in range(3)]
    movers = [shifts(c[2]) for c in cs]
    c_up, c_down = [constants(sub, [rows.get(r) for r in range(8)]) for rows in (UP, DOWN)]
    c_end = [jnp.where(lane >= 64, a, b) for a, b in zip(c_up, c_down)]
    z_low = WHERE[0, 0, 1][2]["Z"]
    z_high = WHERE[0, 0, -1][2]["Z"]
    for t in range(3):
        merged = jnp.where(low4, recv[z_low + 8 * t : z_low + 8 * t + 8, :], recv[z_high + 8 * t : z_high + 8 * t + 8, :])
        for s in range(16):
            ends[16 * t + s] = unpack(merged, s)

    def own_columns(x, carry):
        for y in range(BY):
            i = x * BY + y
            rho, flag = col[i, RHO : RHO + 1, :], col[i, FLAG : FLAG + 1, :]
            u = [col[i, VEL + a : VEL + a + 1, :] for a in range(3)]
            f = [force[a, x + 1, y : y + 1, 0:128] for a in range(3)]
            fz = [force[a, x + 1, y : y + 1, 128:256] for a in range(3)]
            uz = [ext[a, x + 4, y : y + 1, 128:256] for a in range(3)]
            rho_z, flag_z = ends[36 + x, y : y + 1, :], ends[42 + x, y : y + 1, :]
            rz = collide(ends[i], c_end, rho_z, uz, fz)
            sz = jnp.where(flag_z > 0.5, rz, wall)
            for k in range(3):
                r = collide(col[i, 8 * k : 8 * k + 8, :], cs[k], rho, u, f)
                raw[i, 8 * k : 8 * k + 8, :] = r
                s = jnp.where(flag > 0.5, r, wall)
                moved[x + 1, y + 1, 8 * k : 8 * k + 8, :] = movers[k](s, sz)
        return carry

    for x in range(BX):
        own_columns(x, 0)

    for face, (rows, r_rho, r_flag) in FACE.items():
        dx, dy = face
        numbers = [rows.get(r) for r in range(8)]
        c = constants(sub, numbers)
        mover = shifts(c[2])
        ring = WHERE[dx, dy, 0][2]["R"]
        count = 1 if dx and dy else 6
        if count == 6:
            if dx:
                z = [WHERE[dx, 0, s][2]["Z"] for s in (1, -1)]
                slot = 12
            else:
                z = [WHERE[0, dy, s][2]["Z"] + 8 for s in (1, -1)]
                slot = 2
            pz = jnp.where(low4, recv[z[0] : z[0] + 8, :], recv[z[1] : z[1] + 8, :])
            tz = [unpack(pz, slot + t) for t in range(3)]
            cz = (float(dx), float(dy), side, 1.0 / 36.0)
        for j in range(count):
            x = {1: -1, -1: 6, 0: j}[dx]
            y = {1: -1, -1: 6, 0: j}[dy]
            t = recv[ring + 8 * j : ring + 8 * j + 8, :]
            rho, flag = t[r_rho : r_rho + 1], t[r_flag : r_flag + 1]
            yu, yf = y % 16, y % 8
            if count == 6:
                u = [ext[a, x + 4, yu : yu + 1, 0:128] for a in range(3)]
            else:
                u = [t[EDGE_VEL + a : EDGE_VEL + a + 1] for a in range(3)]
            f = [force[a, x + 1, yf : yf + 1, 0:128] for a in range(3)]
            s = jnp.where(flag > 0.5, collide(t, c, rho, u, f), wall)
            if count == 6:
                uz = [ext[a, x + 4, yu : yu + 1, 128:256] for a in range(3)]
                fz = [force[a, x + 1, yf : yf + 1, 128:256] for a in range(3)]
                rz = collide(tz[0][j : j + 1], cz, tz[1][j : j + 1], uz, fz)
                sz = jnp.where(tz[2][j : j + 1] > 0.5, rz, wall[0:1])
                s = mover(s, sz)
            for k in sorted({q // 8 for q in rows.values()}):
                out = None
                for shift in sorted({(q - r) % 8 for r, q in rows.items() if q // 8 == k}):
                    tile = roll(s, shift, 0)
                    members = [q % 8 for r, q in rows.items() if q // 8 == k and (q - r) % 8 == shift]
                    out = tile if out is None else jnp.where(bits(sub, members), tile, out)
                moved[x + 1, y + 1, 8 * k : 8 * k + 8, :] = out

    odd = (iota((24, 128), 0) & 1) == 1
    start = iota((24, 128), 0) == 0

    def passing(x, carry):
        for y in range(BY):
            i = x * BY + y
            r = raw[i]
            turned = jnp.where(start, r, jnp.where(odd, roll(r, 23, 0), roll(r, 1, 0)))
            for k in range(3):
                sources = {}
                for q in natural_numbers(k):
                    if q is not None:
                        sources.setdefault(LATTICE[q][:2], []).append(q % 8)
                out = None
                for (cx, cy), members in sources.items():
                    tile = moved[x + 1 - cx, y + 1 - cy, 8 * k : 8 * k + 8, :]
                    out = tile if out is None else jnp.where(bits(sub, members), tile, out)
                out = jnp.where(out == out, out, turned[8 * k : 8 * k + 8])
                last = min(8 * k + 8, 19)
                nxt[i, 8 * k : last, :] = out[0 : last - 8 * k]
        return carry

    for x in range(BX):
        passing(x, 0)


def finish(col, vel, ownf, recv, wxy, w_hi, w_lo, occ, nxt, vtx, ext, force, raw, moved, ends):
    lane = iota((8, 128), 1)
    sub = iota((8, 128), 0)
    alive = (occ[...] > 0).astype(F32)
    assemble(recv, vel, ext, lane, sub)
    forces(recv, ownf, force)
    step_nodes(col, recv, ext, force, raw, moved, ends, nxt, lane, sub)
    interpolate(ext, wxy, w_hi, w_lo, alive, vtx)


def on_device(sizes, populations, fluid_mask, stencil_base, offsets, occupied_cell_slots, triangles):
    pops = jnp.transpose(populations, (1, 2, 0, 3)).reshape(BX * BY, 19, BZ)
    base = stencil_base.reshape(3, 1, NV)
    off = offsets.reshape(3, 1, NV)
    occ = occupied_cell_slots.reshape(1, 1)
    vmem = pl.BlockSpec(memory_space=pltpu.VMEM)
    hbm = pl.BlockSpec(memory_space=pltpu.HBM)
    shape = jax.ShapeDtypeStruct
    dma = pltpu.SemaphoreType.DMA
    vm = pltpu.VMEM
    middle = pl.pallas_call(
        functools.partial(send_all, sizes),
        name="cells_and_halo",
        out_shape=(
            shape((36, 24, 128), F32),
            shape((3, 6, 8, 128), F32),
            shape((32, 128), F32),
            shape((ROWS, 128), F32),
            shape((32, VP), F32),
            shape((256, VP), BF16),
            shape((256, VP), BF16),
        ),
        in_specs=[hbm, hbm, hbm, hbm, vmem, hbm],
        out_specs=(vmem,) * 7,
        scratch_shapes=[
            vm((ROWS, 128), F32),
            vm((6, 8, 128), I32),
            vm((3, 1, NV), I32),
            vm((3, 1, NV), F32),
            vm((3, NT), I32),
            vm((8, VP), I32),
            vm((8, VP), F32),
            vm((VP, NT), BF16),
            vm((384, VP), F32),
            vm((192, VP), F32),
            vm((24, 128), F32),
            vm((6, 8, 128), F32),
            dma((5,)),
            dma((26,)),
            dma((26,)),
            dma((26,)),
            dma((26,)),
        ],
        compiler_params=pltpu.CompilerParams(collective_id=0, has_side_effects=True, vmem_limit_bytes=48 << 20),
    )(*(pltpu.with_memory_space_constraint(a, pltpu.HBM) for a in (pops, fluid_mask, base, off)), occ, pltpu.with_memory_space_constraint(triangles.T, pltpu.HBM))
    nxt, vtx = pl.pallas_call(
        finish,
        name="collide_and_pass",
        out_shape=(shape((36, 19, 128), F32), shape((3, 1, NV), F32)),
        in_specs=[vmem] * 8,
        out_specs=(vmem, vmem),
        scratch_shapes=[
            vm((3, 14, 16, 256), F32),
            vm((3, 8, 8, 256), F32),
            vm((36, 24, 128), F32),
            vm((8, 8, 24, 128), F32),
            vm((48, 8, 128), F32),
        ],
        compiler_params=pltpu.CompilerParams(vmem_limit_bytes=48 << 20),
    )(*middle, occ)
    nxt = jnp.transpose(nxt.reshape(BX, BY, 19, BZ), (2, 0, 1, 3))
    return nxt, vtx.reshape(1, 1, 1, 3, NV)


def solution(mesh):
    sizes = tuple(mesh.shape[a] for a in AXES)
    placed = (
        P(None, "gx", "gy", "gz"),
        P("gx", "gy", "gz"),
        P("gx", "gy", "gz", None, None),
        P("gx", "gy", "gz", None, None),
        P("gx", "gy", "gz"),
        P(),
    )
    return jax.shard_map(
        functools.partial(on_device, sizes),
        mesh=mesh,
        in_specs=placed,
        out_specs=(P(None, "gx", "gy", "gz"), P("gx", "gy", "gz", None, None)),
        check_vma=False,
    )
```

time: 31.1 us -> 31.4 us (level)
  the two profiles are of different devices: /device:TPU:47 before, /device:TPU:63 now
where the time goes in v3:
time: 31.4 us; the launch traced here: 31.3 us
  Pallas kernels  30 us (96%)
  between operations  1.29 us (4%)
    pallas_call x1, Pallas kernels, on_device(): pl.pallas_call(functools.partial(send_all, sizes), name='cells_and_halo',...  26.9 us
    pallas_call x1, Pallas kernels, on_device(): pl.pallas_call(finish, name='collide_and_pass', out_shape=(shape((36, 19,...  3.03 us

profile of v3, /device:TPU:63, one launch (start us, length us, event | category | flops | bytes accessed | tf_op | source)
XLA Modules:
  0.0 31.3 jit_solution(351056257062359189)
XLA Ops:
  1.3 26.9 %cells_and_halo.1 = (f32[36,24,128]{2,1,0:T(8,128)S(1)}, f32[3,6,8,128]{3,2,1,0:T(8,128)S(1)}, f32[32,128]{1,0:T(8,128)S(1)}, f32[1296,128]{1,0:T(8,128)S(1)}, f...) custom-call(f32[36,19,128]{2,1,0:T(8,128)} %bitcast.15, s32[6,6,128]{2,1,0:T(8,128)} %mask.1, ...), custom_call_target="tpu_custom_call" | custom-call | tf_op jit(solution)/shard_map/cells_and_halo/pallas_call | solution.py:782
  28.2 3.0 %collide_and_pass.1 = (f32[36,19,128]{2,1,0:T(8,128)}, f32[3,1,642]{2,1,0:T(1,128)}) custom-call(f32[36,24,128]{2,1,0:T(8,128)S(1)} %get-tuple-element.11.col, f32[3,6,8,128]{3,2,1,0:T(8,128)S(1)} %get-tuple-element.12.vel, f32[32,128]{1,0:T(8,128)S(1)} %get-tuple-element.13.ownf, f32[1296,128]{1,0:T(8,128)S(1)} %get-tuple-element.14.recv, ...), custom_call_target="tpu_custom_call" | custom-call | tf_op jit(solution)/shard_map/collide_and_pass/pallas_call | solution.py:817

commit v4 on v3

--- a/solution.py
+++ b/solution.py
@@ -67,13 +67,16 @@
     for d in TRAVELS:
         dx, dy, dz = d
         rows = {}
+        if dx and dy and dz == 0:
+            rows["R"] = 8
+        if dx and dz:
+            rows["Z"] = 8
         rows["F"] = (16 if dz == 0 else 8) * (2 if dx == 0 else 1)
         if dz == 0:
-            rows["R"] = 8 if dx and dy else 48
+            if not (dx and dy):
+                rows["R"] = 48
             rows["U"] = 48 if dx and dy else 72
-        elif dx:
-            rows["Z"] = 8
-        else:
+        elif dx == 0:
             rows["Z"] = 16 if dy else 40
         spot, begin = {}, row
         for part, count in rows.items():
@@ -84,6 +87,7 @@
 
 
 WHERE, ROWS = layout()
+USED = {16: 11, 8: 5}
 
 
 def iota(shape, axis):
@@ -212,9 +216,9 @@
 def spread_own(base_s, off_s, loads, outer, mid):
     base, frac = base_s[...], off_s[...]
     four = [four_weights(frac, a) for a in range(3)]
-    low = base[2:3, 0:1] - 6
+    low = jnp.min(jnp.where(base[2:3] > FAR // 2, base[2:3], 1 << 20), axis=1, keepdims=True)
     k = iota((32, 1), 0)
-    z = jnp.where(k < 16, low + k, jnp.where(k < 24, 127 - 16 + k, -7 - 24 + k))
+    z = jnp.where(k < 16, low + k, jnp.where(k < 24, 127 - 16 + k, -4 - 24 + k))
     wz = node_weights(z, base[2:3], four[2])
     left = jnp.concatenate([wz * loads[c : c + 1] for c in range(3)], axis=0)
     wx = node_weights(iota((16, 1), 0) - 4, base[0:1], four[0])
@@ -417,9 +421,6 @@
             i = x * BY + (5 if dy == 1 else 0)
             send[r : r + 8, :] = ring_tile(i, (dx, dy))
             send[r + EDGE_VEL : r + EDGE_VEL + 3, :] = col[i, VEL : VEL + 3, :]
-            u = WHERE[dx, dy, 0][2]["U"]
-            for t, tile in enumerate(paired(tiles, 2, dy, sub)):
-                send[u + 8 * t : u + 8 * t + 8, :] = tile
     for dy in (1, -1):
         u, r = WHERE[0, dy, 0][2]["U"], WHERE[0, dy, 0][2]["R"]
         y = 5 if dy == 1 else 0
@@ -464,23 +465,26 @@
     faces = [d for d in TRAVELS if sum(map(abs, d)) == 1]
     edges = [d for d in TRAVELS if d[0] and d[1] and d[2] == 0]
 
-    early = faces + edges
 
     def fields(d):
+        dx, dy, dz = d
         begin, rows, spot = WHERE[d]
-        row = spot["Z"] if d[2] else spot["U"] if d in edges else spot["R"]
-        src = WHERE[0, 0, 1][2]["Z"] if d[2] else row
-        return copy(src, row, begin + rows - row, d, (send_sem, recv_sem), TRAVELS.index(d))
+        t = TRAVELS.index(d)
+        if d in edges:
+            return copy(spot["U"], spot["U"], 48, (0, dy, 0), (send_sem, recv_sem), t)
+        row = spot["Z"] if dz else spot["R"]
+        src = WHERE[0, 0, 1][2]["Z"] if dz else row
+        return copy(src, row, begin + rows - row, d, (send_sem, recv_sem), t)
 
     def force_copy(d):
         begin, rows, spot = WHERE[d]
-        if d in faces:
+        if d[0]:
+            rows = spot["F"] - begin + USED[8 if d[2] else 16]
+        elif d in faces:
             rows = spot["Z" if d[2] else "R"] - begin
-        elif d in edges:
-            rows = 24
         return copy(begin, begin, rows, d, (fsend_sem, frecv_sem), TRAVELS.index(d))
 
-    for d in early:
+    for d in faces:
 
         @pl.when(present(sizes, me, d))
         def _():
@@ -507,12 +511,38 @@
 
     prepare(base_s, off_s, wxy, w_hi, w_lo)
 
+    def forward(dx):
+        @pl.when(present(sizes, me, (-dx, 0, 0)))
+        def _():
+            fields((dx, 0, 0)).wait_recv()
+            tiles = face_tiles(recv, WHERE[dx, 0, 0][2]["U"], sub)
+            for dy in (1, -1):
+                u = WHERE[dx, dy, 0][2]["U"]
+                for t, tile in enumerate(paired(tiles, 2, dy, sub)):
+                    send[u + 8 * t : u + 8 * t + 8, :] = tile
+
+                @pl.when(present(sizes, me, (-dx, dy, 0)))
+                def _():
+                    fields((dx, dy, 0)).start()
+
+    low_half = me[0] < sizes[0] // 2
+
+    @pl.when(low_half)
+    def _():
+        forward(1)
+        forward(-1)
+
+    @pl.when(jnp.logical_not(low_half))
+    def _():
+        forward(-1)
+        forward(1)
+
     for d in TRAVELS:
 
         @pl.when(present(sizes, me, back(d)))
         def _():
             force_copy(d).wait_recv()
-            if d in early:
+            if d in edges or (d in faces and d[0] == 0):
                 fields(d).wait_recv()
 
     for d in TRAVELS:
@@ -520,7 +550,13 @@
         @pl.when(present(sizes, me, d))
         def _():
             force_copy(d).wait_send()
-            if d in early:
+            if d in faces:
+                fields(d).wait_send()
+
+        if d in edges:
+
+            @pl.when(present(sizes, me, (-d[0], d[1], 0)))
+            def _():
                 fields(d).wait_send()
 
 
@@ -556,11 +592,13 @@
             tile = ref[f : f + kn, :]
             if sx == 0:
                 tile = jnp.concatenate([tile, ref[f + kn : f + 2 * kn, :]], axis=1)
+            else:
+                tile = jnp.where(iota((kn, 128), 0) < USED[kn], tile, 0.0)
             parts.append(tile)
             if sz == 0:
                 zs.append(tile[:, 120:121] if sx else tile[:, 192:193])
             else:
-                zs.append(k8 + (-1.0 if sz == -1 else 121.0))
+                zs.append(k8 + (-1.0 if sz == -1 else 124.0))
         g = jnp.concatenate(parts, axis=0)
         z = jnp.concatenate(zs, axis=0)
         place = jnp.where(z == zl, 1.0, 0.0).astype(BF16)

time: 31.4 us -> 29.2 us (0.930)
  Pallas kernels: 30 us -> 27.8 us
    pallas_call x1, Pallas kernels: 26.9 us -> 24.7 us  [on_device(): pl.pallas_call(functools.partial(send_all, sizes), name='cells_and_halo',...]
where the time goes in v4:
time: 29.2 us; the launch traced here: 29 us
  Pallas kernels  27.8 us (95%)
  between operations  1.29 us (4%)
    pallas_call x1, Pallas kernels, on_device(): pl.pallas_call(functools.partial(send_all, sizes), name='cells_and_halo',...  24.7 us
    pallas_call x1, Pallas kernels, on_device(): pl.pallas_call(finish, name='collide_and_pass', out_shape=(shape((36, 19,...  3.03 us

profile of v4, /device:TPU:63, one launch (start us, length us, event | category | flops | bytes accessed | tf_op | source)
XLA Modules:
  0.0 29.0 jit_solution(13930564320684983378)
XLA Ops:
  1.3 24.7 %cells_and_halo.1 = (f32[36,24,128]{2,1,0:T(8,128)S(1)}, f32[3,6,8,128]{3,2,1,0:T(8,128)S(1)}, f32[32,128]{1,0:T(8,128)S(1)}, f32[1296,128]{1,0:T(8,128)S(1)}, f...) custom-call(f32[36,19,128]{2,1,0:T(8,128)} %bitcast.15, s32[6,6,128]{2,1,0:T(8,128)} %mask.1, ...), custom_call_target="tpu_custom_call" | custom-call | tf_op jit(solution)/shard_map/cells_and_halo/pallas_call | solution.py:820
  26.0 3.0 %collide_and_pass.1 = (f32[36,19,128]{2,1,0:T(8,128)}, f32[3,1,642]{2,1,0:T(1,128)}) custom-call(f32[36,24,128]{2,1,0:T(8,128)S(1)} %get-tuple-element.11.col, f32[3,6,8,128]{3,2,1,0:T(8,128)S(1)} %get-tuple-element.12.vel, f32[32,128]{1,0:T(8,128)S(1)} %get-tuple-element.13.ownf, f32[1296,128]{1,0:T(8,128)S(1)} %get-tuple-element.14.recv, ...), custom_call_target="tpu_custom_call" | custom-call | tf_op jit(solution)/shard_map/collide_and_pass/pallas_call | solution.py:855

commit v5 on v4

--- a/solution.py
+++ b/solution.py
@@ -69,15 +69,13 @@
         rows = {}
         if dx and dy and dz == 0:
             rows["R"] = 8
-        if dx and dz:
-            rows["Z"] = 8
         rows["F"] = (16 if dz == 0 else 8) * (2 if dx == 0 else 1)
         if dz == 0:
             if not (dx and dy):
                 rows["R"] = 48
             rows["U"] = 48 if dx and dy else 72
-        elif dx == 0:
-            rows["Z"] = 16 if dy else 40
+        else:
+            rows["Z"] = 8 if dx else 16 if dy else 40
         spot, begin = {}, row
         for part, count in rows.items():
             spot[part] = row
@@ -411,11 +409,6 @@
             send[t : t + 8, :] = jnp.where(sub < 6, vel[a, xs[j]], roll(vel[a, xs[3]], 6 - 2 * j, 0))
         for y in range(6):
             send[r + 8 * y : r + 8 * y + 8, :] = ring_tile(x * BY + y, (dx, 0))
-        tiles = [vel[a, k] for a in range(3) for k in xs] + ends_of(edge_s, dx, 0, lambda j: x * BY + j)
-        packed = pack(tiles, lane)
-        for dy, dz in itertools.product((0, 1, -1), (1, -1)):
-            z = WHERE[dx, dy, dz][2]["Z"]
-            send[z : z + 8, :] = packed
         for dy in (1, -1):
             r = WHERE[dx, dy, 0][2]["R"]
             i = x * BY + (5 if dy == 1 else 0)
@@ -463,14 +456,16 @@
         )
 
     faces = [d for d in TRAVELS if sum(map(abs, d)) == 1]
-    edges = [d for d in TRAVELS if d[0] and d[1] and d[2] == 0]
+    relayed = [d for d in TRAVELS if d[0] and (d[1] or d[2])]
 
 
     def fields(d):
         dx, dy, dz = d
         begin, rows, spot = WHERE[d]
         t = TRAVELS.index(d)
-        if d in edges:
+        if d in relayed and dz:
+            return copy(WHERE[dx, 0, 1][2]["Z"], spot["Z"], 8, (0, dy, dz), (send_sem, recv_sem), t)
+        if d in relayed:
             return copy(spot["U"], spot["U"], 48, (0, dy, 0), (send_sem, recv_sem), t)
         row = spot["Z"] if dz else spot["R"]
         src = WHERE[0, 0, 1][2]["Z"] if dz else row
@@ -520,10 +515,23 @@
                 u = WHERE[dx, dy, 0][2]["U"]
                 for t, tile in enumerate(paired(tiles, 2, dy, sub)):
                     send[u + 8 * t : u + 8 * t + 8, :] = tile
-
-                @pl.when(present(sizes, me, (-dx, dy, 0)))
-                def _():
-                    fields((dx, dy, 0)).start()
+            rows, r_rho, r_flag = FACE[dx, 0]
+            ring, z = WHERE[dx, 0, 0][2]["R"], WHERE[dx, 0, 1][2]["Z"]
+            row_of = {q: r for r, q in rows.items()}
+            up, down = row_of[NUMBER[dx, 0, 1]], row_of[NUMBER[dx, 0, -1]]
+            edge_s[...] = jnp.zeros((24, 128), F32)
+            for y in range(6):
+                t = recv[ring + 8 * y : ring + 8 * y + 8, :]
+                edge_s[y : y + 1, :] = jnp.where(lane[0:1] >= 64, t[up : up + 1], t[down : down + 1])
+                edge_s[8 + y : 9 + y, :] = t[r_rho : r_rho + 1]
+                edge_s[16 + y : 17 + y, :] = t[r_flag : r_flag + 1]
+            send[z : z + 8, :] = pack(tiles + [edge_s[8 * t : 8 * t + 8, :] for t in range(3)], lane)
+            for d in relayed:
+                if d[0] == dx:
+
+                    @pl.when(present(sizes, me, (-dx, d[1], d[2])))
+                    def _():
+                        fields(d).start()
 
     low_half = me[0] < sizes[0] // 2
 
@@ -542,7 +550,7 @@
         @pl.when(present(sizes, me, back(d)))
         def _():
             force_copy(d).wait_recv()
-            if d in edges or (d in faces and d[0] == 0):
+            if d in relayed or (d in faces and d[0] == 0):
                 fields(d).wait_recv()
 
     for d in TRAVELS:
@@ -553,9 +561,9 @@
             if d in faces:
                 fields(d).wait_send()
 
-        if d in edges:
-
-            @pl.when(present(sizes, me, (-d[0], d[1], 0)))
+        if d in relayed:
+
+            @pl.when(present(sizes, me, (-d[0], d[1], d[2])))
             def _():
                 fields(d).wait_send()
 

time: 29.2 us -> 30.2 us (1.034)
  Pallas kernels: 27.8 us -> 28.8 us
    pallas_call x1, Pallas kernels: 24.7 us -> 25.7 us  [on_device(): pl.pallas_call(functools.partial(send_all, sizes), name='cells_and_halo',...]
where the time goes in v5:
time: 30.2 us; the launch traced here: 30.1 us
  Pallas kernels  28.8 us (95%)
  between operations  1.29 us (4%)
    pallas_call x1, Pallas kernels, on_device(): pl.pallas_call(functools.partial(send_all, sizes), name='cells_and_halo',...  25.7 us
    pallas_call x1, Pallas kernels, on_device(): pl.pallas_call(finish, name='collide_and_pass', out_shape=(shape((36, 19,...  3.04 us

profile of v5, /device:TPU:63, one launch (start us, length us, event | category | flops | bytes accessed | tf_op | source)
XLA Modules:
  0.0 30.1 jit_solution(13038130017072836553)
XLA Ops:
  1.3 25.7 %cells_and_halo.1 = (f32[36,24,128]{2,1,0:T(8,128)S(1)}, f32[3,6,8,128]{3,2,1,0:T(8,128)S(1)}, f32[32,128]{1,0:T(8,128)S(1)}, f32[1296,128]{1,0:T(8,128)S(1)}, f...) custom-call(f32[36,19,128]{2,1,0:T(8,128)} %bitcast.15, s32[6,6,128]{2,1,0:T(8,128)} %mask.1, ...), custom_call_target="tpu_custom_call" | custom-call | tf_op jit(solution)/shard_map/cells_and_halo/pallas_call | solution.py:828
  27.0 3.0 %collide_and_pass.1 = (f32[36,19,128]{2,1,0:T(8,128)}, f32[3,1,642]{2,1,0:T(1,128)}) custom-call(f32[36,24,128]{2,1,0:T(8,128)S(1)} %get-tuple-element.11.col, f32[3,6,8,128]{3,2,1,0:T(8,128)S(1)} %get-tuple-element.12.vel, f32[32,128]{1,0:T(8,128)S(1)} %get-tuple-element.13.ownf, f32[1296,128]{1,0:T(8,128)S(1)} %get-tuple-element.14.recv, ...), custom_call_target="tpu_custom_call" | custom-call | tf_op jit(solution)/shard_map/collide_and_pass/pallas_call | solution.py:863

commit v6 on v4

--- a/solution.py
+++ b/solution.py
@@ -173,11 +173,14 @@
 
 
 def incidence_of(tri, incidence):
+    vertex = iota((16, NT), 0).astype(jnp.int16)
+    one, none = jnp.ones((16, NT), BF16), jnp.zeros((16, NT), BF16)
+
     def fill(step, carry):
         rows = pl.multiple_of(step * 16, 16)
-        vertex = iota((16, NT), 0) + rows
-        hit = (vertex == tri[0:1]) | (vertex == tri[1:2]) | (vertex == tri[2:3])
-        incidence[pl.ds(rows, 16), :] = jnp.where(hit, 1.0, 0.0).astype(BF16)
+        t = [jnp.broadcast_to(tri[a : a + 1] - rows, (16, NT)).astype(jnp.int16) for a in range(3)]
+        hit = (vertex == t[0]) | (vertex == t[1]) | (vertex == t[2])
+        incidence[pl.ds(rows, 16), :] = jnp.where(hit, one, none)
         return carry
 
     lax.fori_loop(0, 41, fill, 0)
@@ -339,7 +342,7 @@
 
     barrier = pltpu.get_barrier_semaphore()
     count = jnp.int32(0)
-    for d in TRAVELS:
+    for d in sorted(TRAVELS, key=lambda d: d[1]):
         ok = present(sizes, me, d)
         count = count + ok.astype(I32)
 
@@ -400,8 +403,6 @@
             edge_s[16 + j : 17 + j, :] = col[i, FLAG : FLAG + 1, :]
         return [edge_s[8 * t : 8 * t + 8, :] for t in range(3)]
 
-    us = [vel[a, x] for a in range(3) for x in range(6)]
-    first = pack(us[:16], lane)
     for dx in (1, -1):
         u, r = WHERE[dx, 0, 0][2]["U"], WHERE[dx, 0, 0][2]["R"]
         xs = range(2, 6) if dx == 1 else range(4)
@@ -411,6 +412,55 @@
             send[t : t + 8, :] = jnp.where(sub < 6, vel[a, xs[j]], roll(vel[a, xs[3]], 6 - 2 * j, 0))
         for y in range(6):
             send[r + 8 * y : r + 8 * y + 8, :] = ring_tile(x * BY + y, (dx, 0))
+    load_vertices(base_v, off_v, base_s, off_s)
+    alive = (occ[...] > 0).astype(F32)
+    incidence_of(tri_v, incidence)
+    pl.semaphore_wait(barrier, count)
+
+    def copy(src, dst, rows, to, sems, t):
+        return pltpu.make_async_remote_copy(
+            src_ref=send.at[pl.ds(src, rows)],
+            dst_ref=recv.at[pl.ds(dst, rows)],
+            send_sem=sems[0].at[t],
+            recv_sem=sems[1].at[t],
+            device_id=at(to),
+            device_id_type=MESH,
+        )
+
+    faces = [d for d in TRAVELS if sum(map(abs, d)) == 1]
+    edges = [d for d in TRAVELS if d[0] and d[1] and d[2] == 0]
+
+
+    def fields(d):
+        dx, dy, dz = d
+        begin, rows, spot = WHERE[d]
+        t = TRAVELS.index(d)
+        if d in edges:
+            return copy(spot["U"], spot["U"], 48, (0, dy, 0), (send_sem, recv_sem), t)
+        row = spot["Z"] if dz else spot["R"]
+        src = WHERE[0, 0, 1][2]["Z"] if dz else row
+        return copy(src, row, begin + rows - row, d, (send_sem, recv_sem), t)
+
+    def force_copy(d):
+        begin, rows, spot = WHERE[d]
+        if d[0]:
+            rows = spot["F"] - begin + USED[8 if d[2] else 16]
+        elif d in faces:
+            rows = spot["Z" if d[2] else "R"] - begin
+        return copy(begin, begin, rows, d, (fsend_sem, frecv_sem), TRAVELS.index(d))
+
+    for d in faces:
+        if d[0]:
+
+            @pl.when(present(sizes, me, d))
+            def _():
+                fields(d).start()
+
+    us = [vel[a, x] for a in range(3) for x in range(6)]
+    first = pack(us[:16], lane)
+    for dx in (1, -1):
+        xs = range(2, 6) if dx == 1 else range(4)
+        x = 5 if dx == 1 else 0
         tiles = [vel[a, k] for a in range(3) for k in xs] + ends_of(edge_s, dx, 0, lambda j: x * BY + j)
         packed = pack(tiles, lane)
         for dy, dz in itertools.product((0, 1, -1), (1, -1)):
@@ -447,48 +497,12 @@
     for t in range(5):
         send[z + 8 * t : z + 8 * t + 8, :] = pack(tiles[16 * t : 16 * t + 16], lane)
 
-    load_vertices(base_v, off_v, base_s, off_s)
-    alive = (occ[...] > 0).astype(F32)
-    incidence_of(tri_v, incidence)
-    pl.semaphore_wait(barrier, count)
-
-    def copy(src, dst, rows, to, sems, t):
-        return pltpu.make_async_remote_copy(
-            src_ref=send.at[pl.ds(src, rows)],
-            dst_ref=recv.at[pl.ds(dst, rows)],
-            send_sem=sems[0].at[t],
-            recv_sem=sems[1].at[t],
-            device_id=at(to),
-            device_id_type=MESH,
-        )
-
-    faces = [d for d in TRAVELS if sum(map(abs, d)) == 1]
-    edges = [d for d in TRAVELS if d[0] and d[1] and d[2] == 0]
-
-
-    def fields(d):
-        dx, dy, dz = d
-        begin, rows, spot = WHERE[d]
-        t = TRAVELS.index(d)
-        if d in edges:
-            return copy(spot["U"], spot["U"], 48, (0, dy, 0), (send_sem, recv_sem), t)
-        row = spot["Z"] if dz else spot["R"]
-        src = WHERE[0, 0, 1][2]["Z"] if dz else row
-        return copy(src, row, begin + rows - row, d, (send_sem, recv_sem), t)
-
-    def force_copy(d):
-        begin, rows, spot = WHERE[d]
-        if d[0]:
-            rows = spot["F"] - begin + USED[8 if d[2] else 16]
-        elif d in faces:
-            rows = spot["Z" if d[2] else "R"] - begin
-        return copy(begin, begin, rows, d, (fsend_sem, frecv_sem), TRAVELS.index(d))
-
     for d in faces:
-
-        @pl.when(present(sizes, me, d))
-        def _():
-            fields(d).start()
+        if d[0] == 0:
+
+            @pl.when(present(sizes, me, d))
+            def _():
+                fields(d).start()
 
     loads = membrane(base_s, off_s, alive, incidence)
     f_outer, f_mid, z16 = spread_own(base_s, off_s, loads, outer, mid)

time: 29.2 us -> 29.2 us (level)
  no operation moved by 1% of the time
where the time goes in v6:
time: 29.2 us; the launch traced here: 29 us
  Pallas kernels  27.8 us (95%)
  between operations  1.29 us (4%)
    pallas_call x1, Pallas kernels, on_device(): pl.pallas_call(functools.partial(send_all, sizes), name='cells_and_halo',...  24.7 us
    pallas_call x1, Pallas kernels, on_device(): pl.pallas_call(finish, name='collide_and_pass', out_shape=(shape((36, 19,...  3.03 us

profile of v6, /device:TPU:63, one launch (start us, length us, event | category | flops | bytes accessed | tf_op | source)
XLA Modules:
  0.0 29.0 jit_solution(16819810585524553613)
XLA Ops:
  1.3 24.7 %cells_and_halo.1 = (f32[36,24,128]{2,1,0:T(8,128)S(1)}, f32[3,6,8,128]{3,2,1,0:T(8,128)S(1)}, f32[32,128]{1,0:T(8,128)S(1)}, f32[1296,128]{1,0:T(8,128)S(1)}, f...) custom-call(f32[36,19,128]{2,1,0:T(8,128)} %bitcast.15, s32[6,6,128]{2,1,0:T(8,128)} %mask.1, ...), custom_call_target="tpu_custom_call" | custom-call | tf_op jit(solution)/shard_map/cells_and_halo/pallas_call | solution.py:834
  26.0 3.0 %collide_and_pass.1 = (f32[36,19,128]{2,1,0:T(8,128)}, f32[3,1,642]{2,1,0:T(1,128)}) custom-call(f32[36,24,128]{2,1,0:T(8,128)S(1)} %get-tuple-element.11.col, f32[3,6,8,128]{3,2,1,0:T(8,128)S(1)} %get-tuple-element.12.vel, f32[32,128]{1,0:T(8,128)S(1)} %get-tuple-element.13.ownf, f32[1296,128]{1,0:T(8,128)S(1)} %get-tuple-element.14.recv, ...), custom_call_target="tpu_custom_call" | custom-call | tf_op jit(solution)/shard_map/collide_and_pass/pallas_call | solution.py:869
